TPU v7x, 32 devices: a whole 2x2x4 slice. The times are simulated.
32 devices in a mesh: row: 16 (over z, y, core), col: 2 (over x).
Axes of the slice: x: 2, y: 2, z: 4, core: 2. Of those that a mesh axis runs over, the one named last changes fastest.
Arguments:
- features: bfloat16 [4096, 2048], P('col', 'row'), may hold values from -6 to 6
- weight: bfloat16 [2048, 2048], replicated, may hold values from -0.125 to 0.125
- bias: bfloat16 [2048], replicated, may hold values from -3 to 3
- self_scale: float32 [4096], P('row'), may hold values from 0.5 to 2
- adj_tiles: bfloat16 [16, 2, 32, 128, 128], P('row', 'col'), may hold values from 0 to 1, as said below
- tile_ids: int32 [16, 2, 32], P('row', 'col'), may hold values from 0 to 31, as said below
- tile_counts: int32 [16, 2], P('row', 'col'), may hold values from 4 to 32, as said below
- cotangent: bfloat16 [4096, 2048], P(('row', 'col')), may hold values from -6 to 6
Outputs:
- outputs: float32 [4096, 2048], P(('row', 'col'))
- d_features: float32 [4096, 2048], P('col', 'row')
- d_weight: float32 [2048, 2048], replicated
- d_bias: float32 [2048], replicated
Inputs may be any that keep to these rules, and one draw needn't show every extreme that they name: `adj_tiles`: entries are non-negative. `tile_ids`: within a block all 32 ids differ, live or not. `tile_counts`: some block is full in every draw.
All inputs are finite; a program needn't handle non-finite values.
Results may differ from a plain program's by a relative error of at most 0.0055.
Values may be sent and summed in bfloat16 or wider, within the bound.
A program may use at most 320 MiB of HBM per device.

v0:
```python
import jax
import jax.numpy as jnp
from jax import lax
from jax.sharding import PartitionSpec as P


def tile_sweep(tiles, source_ids, target_ids, tile_count, source, target_tiles, flip):
    feature_cols = source.shape[-1]
    source_grid = source.reshape(-1, 128, feature_cols)
    slot_total = tiles.shape[0]
    group_size = min(32, slot_total)
    group_count = (tile_count + group_size - 1) // group_size
    pattern = "tji,tjf->tif" if flip else "tij,tjf->tif"

    def add_group(round_no, running):
        first_slot = jnp.minimum(round_no * group_size, slot_total - group_size)
        tile_group = lax.dynamic_slice_in_dim(tiles, first_slot, group_size, 0)
        from_ids = lax.dynamic_slice_in_dim(source_ids, first_slot, group_size, 0)
        to_ids = lax.dynamic_slice_in_dim(target_ids, first_slot, group_size, 0)
        slot_index = first_slot + jnp.arange(group_size, dtype=jnp.int32)
        live_slot = (slot_index >= round_no * group_size) & (slot_index < tile_count)
        pieces = jnp.take(source_grid, from_ids, axis=0)
        products = jnp.einsum(pattern, tile_group, pieces, preferred_element_type=jnp.float32)
        products = jnp.where(live_slot[:, None, None], products, 0.0)
        return running.at[to_ids].add(products)

    zeros_acc = jnp.zeros((target_tiles, 128, feature_cols), jnp.float32)
    return lax.fori_loop(0, group_count, add_group, zeros_acc).reshape(-1, feature_cols)


def per_device(features, weight, bias, self_scale, adj_tiles, tile_ids, tile_counts, cotangent):
    tiles = adj_tiles[0, 0]
    tile_list = tile_ids[0, 0]
    tile_count = tile_counts[0, 0]
    row_block = self_scale.shape[0]
    col_block = features.shape[0]
    tile_rows = row_block // 128
    tile_cols = col_block // 128
    row_no = lax.axis_index("row")
    col_no = lax.axis_index("col")
    start_row = row_no * row_block
    inside = col_no == start_row // col_block
    offset = jnp.where(inside, start_row - col_no * col_block, 0)
    self_rows = jnp.where(inside, self_scale, 0.0)[:, None]
    col_ids = tile_list % tile_cols
    row_ids = tile_list // tile_cols

    def aggregate_piece(feature_piece):
        summed = tile_sweep(tiles, col_ids, row_ids, tile_count, feature_piece, tile_rows, False)
        return summed + self_rows * lax.dynamic_slice_in_dim(feature_piece, offset, row_block, 0)

    row_terms = aggregate_piece(lax.all_gather(features, "row", axis=1, tiled=True))
    aggregated = lax.psum_scatter(row_terms, "col", scatter_dimension=0, tiled=True)
    kept = aggregated.astype(jnp.bfloat16)
    pre_act = jnp.dot(kept, weight, preferred_element_type=jnp.float32) + bias.astype(jnp.float32)
    sigmoid_val = jax.nn.sigmoid(pre_act)
    outputs = pre_act * sigmoid_val
    again_terms = aggregate_piece(lax.all_gather(features, "row", axis=1, tiled=True))
    layer_in = lax.psum_scatter(again_terms, "col", scatter_dimension=0, tiled=True).astype(
        jnp.bfloat16
    )
    slope = sigmoid_val * (1.0 + pre_act * (1.0 - sigmoid_val))
    d_pre = (cotangent.astype(jnp.float32) * slope).astype(jnp.bfloat16)
    d_weight_part = lax.dot_general(
        layer_in, d_pre, (((0,), (0,)), ((), ())), preferred_element_type=jnp.float32
    )
    d_bias_part = jnp.sum(d_pre.astype(jnp.float32), axis=0)
    d_weight, d_bias = lax.psum((d_weight_part, d_bias_part), ("row", "col"))
    d_layer = lax.dot_general(
        d_pre, weight, (((1,), (1,)), ((), ())), preferred_element_type=jnp.float32
    ).astype(jnp.bfloat16)
    whole_grad = lax.all_gather(d_layer, "col", axis=0, tiled=True)
    spread = tile_sweep(tiles, row_ids, col_ids, tile_count, whole_grad, tile_cols, True)
    own_part = lax.dynamic_slice_in_dim(spread, offset, row_block, 0) + self_rows * whole_grad
    spread = lax.dynamic_update_slice_in_dim(spread, own_part, offset, 0)
    d_features = lax.psum_scatter(spread, "row", scatter_dimension=1, tiled=True)
    return (outputs, d_features, d_weight, d_bias)


def solution(mesh):
    return jax.shard_map(
        per_device,
        mesh=mesh,
        in_specs=(
            P("col", "row"),
            P(),
            P(),
            P("row"),
            P("row", "col", None, None, None),
            P("row", "col", None),
            P("row", "col"),
            P(("row", "col"), None),
        ),
        out_specs=(P(("row", "col"), None), P("col", "row"), P(), P()),
        check_vma=False,
    )
```

profile of v0, /device:TPU:8, one launch (start us, length us, event | category | flops | bytes accessed | tf_op | source)
XLA Modules:
  0.0 743.1 jit_solution(3755336423773579811)
XLA Ops:
  7.2 0.0 all-gather.3.cloned.1.call-start
  7.2 0.7 all-gather.3.cloned.1.call-update
  7.9 0.0 reduce-scatter.3.cloned.1.call-start
  8.6 0.7 and_select_fusion
  9.3 1.3 broadcast_select_fusion
  10.6 77.0 %all-gather.3.cloned.1.call-done = bf16[2048,2048]{1,0:T(8,128)(2,1)} async-done(((bf16[2048,128]{1,0:T(8,128)(2,1)}), bf16[2048,2048]{1,0:T(8,128)(2,1)}) %all-gather.3.cloned.1.call-update) | async-done | bytes 8388624 | tf_op jit(solution)/shard_map/all_gather | solution.py:52
  87.6 0.2 broadcast.124
  87.8 0.0 copy-start.5
  87.8 0.0 copy-start.8
  87.8 101.6 %while.24 = (s32[]{:T(128)}, f32[2,128,2048]{2,1,0:T(8,128)S(1)}, s32[]{:T(128)}, s32[32]{0:T(128)S(1)}, s32[]{:T(128)}, /*index=5*/bf16[16,128,2048]{2,1,0:T(8,...) while((s32[]{:T(128)}, f32[2,128,2048]{2,1,0:T(8,128)S(1)}, ...), condition=%wide.region_2.4_spmd, body=%wide.region_0.3_spmd.sunk | while | flops 2172651008 | bytes 256906544 | solution.py:28
  87.9 0.0 copy-start.1
  87.9 10.9 %gather_fusion = bf16[32,128,2048]{2,1,0:T(8,128)(2,1)} fusion(bf16[16,128,2048]{2,1,0:T(8,128)(2,1)} %get-tuple-element.291, s32[1024]{0:T(1024)S(1)} %pad_clamp_fusion.4), kind=kCustom, calls=%fused_computation.clone.clone.1 | custom fusion | bytes 33554560 | tf_op jit(solution)/shard_map/while/body/jit(_take)/gather | solution.py:22
  98.8 0.7 compare_and_fusion.6
  99.5 0.0 copy-done.1
  99.5 18.2 %select_bitcast_fusion.4 = f32[32,128,2048]{1,2,0:T(8,128)} fusion(bf16[32,128,128]{2,1,0:T(8,128)(2,1)S(1)} %copy-done.1, bf16[32,128,2048]{2,1,0:T(8,128)(2,1)} %gather_fusion, pred[32]{0:T(512)(128)(4,1)S(1)} %get-tuple-element.250, pred[32]{0:T(512)(128)(4,1)S(1)} %get-tuple-element.251), kind=kOutput, calls=%fused_computation.17.clone.1 | convolution fusion | flops 2164260864 | bytes 51380288 | tf_op jit(solution)/shard_map/while/body/tij,tjf->tif/dot_general | solution.py:23
  117.7 33.4 %copy.20 = f32[32,128,2048]{2,1,0:T(8,128)} copy(f32[32,128,2048]{1,2,0:T(8,128)} %select_bitcast_fusion.4) | data formatting | bytes 67108864 | tf_op jit(solution)/shard_map/while/body/jit(_where)/select_n | solution.py:24
  151.1 38.4 %scatter_fusion = f32[2,128,2048]{2,1,0:T(8,128)S(1)} fusion(f32[2,128,2048]{2,1,0:T(8,128)S(1)} %get-tuple-element.276, s32[32]{0:T(128)S(1)} %fusion.29, f32[32,128,2048]{2,1,0:T(8,128)} %copy.20), kind=kCustom, calls=%fused_computation.2.clone.1 | custom fusion | flops 8388608 | bytes 100663424 | tf_op jit(solution)/shard_map/while/body/scatter-add | solution.py:25
  189.5 0.0 copy-done.5
  189.5 3.1 bitcast_add_fusion
  192.6 0.0 reduce-scatter.3.cloned.1.call-update
  192.6 0.0 all-gather.5.cloned.1.call-start
  192.6 0.0 copy-done.8
  192.7 31.8 %reduce-scatter.3.cloned.1.call-done = f32[128,2048]{1,0:T(8,128)} async-done(((f32[256,2048]{1,0:T(8,128)}), f32[128,2048]{1,0:T(8,128)}) %reduce-scatter.3.cloned.1.call-update) | async-done | bytes 1048592 | tf_op jit(solution)/shard_map/reduce_scatter | solution.py:53
  224.5 7.2 convert_reduce_fusion
  231.7 0.0 copy-done.3
  231.7 3.7 convolution_convert_fusion
  235.4 0.0 all-gather.5.cloned.1.call-update
  235.4 0.0 all-reduce.2.cloned.1.call-start
  235.4 0.0 copy-done.4
  235.5 8.4 %fusion.12 = f32[2048,2048]{1,0:T(8,128)} fusion(bf16[128,2048]{1,0:T(8,128)(2,1)S(1)} %get-tuple-element.142, f32[128,2048]{1,0:T(8,128)S(1)} %copy-done.4), kind=kOutput, calls=%fused_computation.36 | convolution fusion | flops 1074003968 | bytes 18350080 | tf_op jit(solution)/shard_map/dot_general | solution.py:64
  243.9 0.0 all-reduce.2.cloned.1.call-update
  243.9 0.2 reduce-scatter.5.cloned.1.call-start
  244.2 12.7 %all-gather.5.cloned.1.call-done = bf16[256,2048]{1,0:T(8,128)(2,1)} async-done(((bf16[128,2048]{1,0:T(8,128)(2,1)}), bf16[256,2048]{1,0:T(8,128)(2,1)}) %all-gather.5.cloned.1.call-update) | async-done | bytes 1048592 | tf_op jit(solution)/shard_map/all_gather | solution.py:72
  256.9 8.3 %broadcast_in_dim.59 = f32[16,128,2048]{2,1,0:T(8,128)} broadcast(f32[]{:T(128)} %constant.114.clone.1), dimensions={} | broadcast | bytes 16777220 | tf_op jit(solution)/shard_map/broadcast_in_dim | solution.py:27
  265.2 0.0 copy-done.2
  265.2 0.0 copy-done
  265.2 130.0 %while.25 = (s32[]{:T(128)}, f32[16,128,2048]{2,1,0:T(8,128)}, s32[]{:T(128)}, s32[32]{0:T(128)S(1)}, s32[]{:T(128)}, /*index=5*/s32[32]{0:T(128)S(1)}, bf16[2,1...) while((s32[]{:T(128)}, f32[16,128,2048]{2,1,0:T(8,128)}, ...), condition=%wide.region_6.8_spmd, body=%wide.region_4.7_spmd.sunk | while | flops 2172651008 | bytes 252712240 | solution.py:28
  265.2 7.7 %gather_fusion.1 = bf16[32,128,2048]{2,1,0:T(8,128)(2,1)} fusion(bf16[2,128,2048]{2,1,0:T(8,128)(2,1)S(1)} %get-tuple-element.325, s32[1024]{0:T(1024)S(1)} %pad_clamp_fusion.5), kind=kCustom, calls=%fused_computation.1.clone.1 | custom fusion | bytes 33554560 | tf_op jit(solution)/shard_map/while/body/jit(_take)/gather | solution.py:22
  272.9 0.7 compare_and_fusion.7
  273.6 19.3 %select_bitcast_fusion.5 = f32[32,128,2048]{1,2,0:T(8,128)} fusion(bf16[32,128,128]{2,1,0:T(8,128)(2,1)S(1)} %get-tuple-element.326, bf16[32,128,2048]{2,1,0:T(8,128)(2,1)} %gather_fusion.1, pred[32]{0:T(512)(128)(4,1)S(1)} %get-tuple-element.262, pred[32]{0:T(512)(128)(4,1)S(1)} %get-tuple-element.263), kind=kOutput, calls=%fused_computation.4.clone.1 | convolution fusion | flops 2164260864 | bytes 51380288 | tf_op jit(solution)/shard_map/while/body/tji,tjf->tif/dot_general | solution.py:23
  292.9 33.8 %copy.21 = f32[32,128,2048]{2,1,0:T(8,128)} copy(f32[32,128,2048]{1,2,0:T(8,128)} %select_bitcast_fusion.5) | data formatting | bytes 67108864 | tf_op jit(solution)/shard_map/while/body/jit(_where)/select_n | solution.py:24
  326.6 68.5 %scatter_fusion.1 = f32[16,128,2048]{2,1,0:T(8,128)} fusion(f32[16,128,2048]{2,1,0:T(8,128)} %get-tuple-element.309, s32[32]{0:T(128)S(1)} %get-tuple-element.260, f32[32,128,2048]{2,1,0:T(8,128)} %copy.21), kind=kCustom, calls=%fused_computation.3.clone.1 | custom fusion | flops 8388608 | bytes 100663424 | tf_op jit(solution)/shard_map/while/body/scatter-add | solution.py:25
  395.1 3.2 add_dynamic-update-slice_fusion
  398.3 0.0 reduce-scatter.5.cloned.1.call-update
  398.4 40.8 %psum.15 = f32[2048]{0:T(1024)} all-reduce(f32[2048]{0:T(1024)S(1)} %copy-done.7), channel_id=1, replica_groups=mesh['row'=16,'col'=2] {'row','col'}, use_global_device_ids=true, to_apply=%region_10.12 | all-reduce | flops 2048 | bytes 16384 | tf_op jit(solution)/shard_map/psum | solution.py:68
  439.2 103.3 %all-reduce.2.cloned.1.call-done = f32[2048,2048]{1,0:T(8,128)} async-done(((f32[2048,2048]{1,0:T(8,128)}), f32[2048,2048]{1,0:T(8,128)}) %all-reduce.2.cloned.1.call-update) | async-done | bytes 16777232 | tf_op jit(solution)/shard_map/psum | solution.py:68
  542.5 182.2 %reduce-scatter.5.cloned.1.call-done = f32[2048,128]{1,0:T(8,128)} async-done(((f32[2048,2048]{1,0:T(8,128)}), f32[2048,128]{1,0:T(8,128)}) %reduce-scatter.5.cloned.1.call-update) | async-done | bytes 1048592 | tf_op jit(solution)/shard_map/reduce_scatter | solution.py:76
  724.7 11.8 %copy.39 = f32[2048,2048]{1,0:T(8,128)} copy(f32[2048,2048]{1,0:T(8,128)} %all-reduce.2.cloned.1.call-done) | data formatting | bytes 33554432
  (14 shorter events, 0.0 us)
Async XLA Ops:
  7.2 80.4 %all-gather.3.cloned.1.call-start = ((), (), s32[]{:S(2)}) async-start(), calls=%async_computation.2 | async-start | bytes 8912896 | tf_op jit(solution)/shard_map/all_gather | solution.py:52
  7.9 216.6 %reduce-scatter.3.cloned.1.call-start = ((), (), s32[]{:S(2)}) async-start(), calls=%async_computation.3 | async-start | bytes 3145728 | tf_op jit(solution)/shard_map/reduce_scatter | solution.py:53
  87.8 101.7 %copy-start.5 = (f32[256]{0:T(256)S(1)}, f32[256]{0:T(256)}, u32[]{:S(2)}) copy-start(f32[256]{0:T(256)} %broadcast_select_fusion) | copy-start | bytes 3076
  87.8 104.8 %copy-start.8 = (bf16[2048]{0:T(1024)(128)(2,1)S(1)}, bf16[2048]{0:T(1024)(128)(2,1)}, u32[]{:S(2)}) copy-start(bf16[2048]{0:T(1024)(128)(2,1)} %param.16) | copy-start | bytes 12292
  87.9 11.6 %copy-start.1 = (bf16[32,128,128]{2,1,0:T(8,128)(2,1)S(1)}, bf16[32,128,128]{2,1,0:T(8,128)(2,1)}, u32[]{:S(2)}) copy-start(bf16[32,128,128]{2,1,0:T(8,128)(2,1)} %get-tuple-element.293) | copy-start | bytes 3145732 | tf_op jit(solution)/shard_map/while
  192.6 64.3 %all-gather.5.cloned.1.call-start = ((), (), s32[]{:S(2)}) async-start(), calls=%async_computation.4 | async-start | bytes 1572864 | tf_op jit(solution)/shard_map/all_gather | solution.py:72
  224.5 7.2 copy-start.3
  224.5 10.9 %copy-start.4 = (f32[128,2048]{1,0:T(8,128)S(1)}, f32[128,2048]{1,0:T(8,128)}, u32[]{:S(2)}) copy-start(f32[128,2048]{1,0:T(8,128)} %reduce-scatter.3.cloned.1.call-done) | copy-start | bytes 3145732
  235.4 307.1 %all-reduce.2.cloned.1.call-start = ((), (), s32[]{:S(2)}) async-start(), calls=%async_computation.6 | async-start | bytes 33554432 | tf_op jit(solution)/shard_map/psum | solution.py:68
  243.9 21.3 %copy-start.2 = (bf16[32,128,128]{2,1,0:T(8,128)(2,1)S(1)}, bf16[32,128,128]{2,1,0:T(8,128)(2,1)}, u32[]{:S(2)}) copy-start(bf16[32,128,128]{2,1,0:T(8,128)(2,1)} %get-tuple-element.345) | copy-start | bytes 3145732
  243.9 480.8 %reduce-scatter.5.cloned.1.call-start = ((), (), s32[]{:S(2)}) async-start(), calls=%async_computation.5 | async-start | bytes 17825792 | tf_op jit(solution)/shard_map/reduce_scatter | solution.py:76
  256.9 8.3 %copy-start = (bf16[256,2048]{1,0:T(8,128)(2,1)S(1)}, bf16[256,2048]{1,0:T(8,128)(2,1)}, u32[]{:S(2)}) copy-start(bf16[256,2048]{1,0:T(8,128)(2,1)} %all-gather.5.cloned.1.call-done) | copy-start | bytes 3145732
  265.2 130.0 %copy-start.6 = (f32[256]{0:T(256)S(1)}, f32[256]{0:T(256)}, u32[]{:S(2)}) copy-start(f32[256]{0:T(256)} %broadcast_select_fusion) | copy-start | bytes 3076
  395.1 3.2 copy-start.7
Sparse Core Ops, SparseCore 0:
  10.2 77.3 all-gather.2
  192.7 31.7 reduce-scatter.2
  235.5 21.2 all-gather.4
  263.8 278.6 all-reduce.1
  547.6 177.0 reduce-scatter.4
where the time goes:
time: 748 us; the launch traced here: 743 us
  waiting for transfers between devices  408 us (55%)
  other arithmetic  116 us (16%)
  local copies, waits for them, and re-layouts  106 us (14%)
  matrix products  56.8 us (8%)
  blocking collectives  40.8 us (5%)
  between operations  14.6 us (2%)
    reduce_scatter x1, waiting for transfers between devices, per_device(): lax.psum_scatter(spread, 'row', scatter_dimension=1, tiled=True)  182 us
    scatter-add x2, other arithmetic, add_group(): return running.at[to_ids].add(products)  107 us
    psum x1, waiting for transfers between devices, per_device(): d_weight, d_bias = lax.psum((d_weight_part, d_bias_part), ('row', 'col'))  103 us
    all_gather x1, waiting for transfers between devices, per_device(): lax.all_gather(features, 'row', axis=1, tiled=True)  77 us
    select_n x2, local copies, waits for them, and re-layouts, add_group(): products = jnp.where(live_slot[:, None, None], products, 0.0)  67.2 us
    psum x1, blocking collectives, per_device(): d_weight, d_bias = lax.psum((d_weight_part, d_bias_part), ('row', 'col'))  40.8 us
    dot_general x2, matrix products, add_group(): jnp.einsum(pattern, tile_group, pieces, preferred_element_type=jnp.float32)  37.5 us
    reduce_scatter x1, waiting for transfers between devices, per_device(): lax.psum_scatter(row_terms, 'col', scatter_dimension=0, tiled=True)  31.8 us
  transfers between devices with their start and end apart: 5, of which 5 were waited for; matrix products, arithmetic and copies ran while one was open for 20% of the time, Pallas kernels for 0%

commit v1 on v0

v1 whole, which is shorter than its diff:
```python
import jax
import jax.numpy as jnp
from jax import lax
from jax.experimental import pallas as pl
from jax.experimental.pallas import tpu as pltpu
from jax.sharding import PartitionSpec as P

MESH = pl.DeviceIdType.MESH
F32 = jnp.float32
BF16 = jnp.bfloat16
MIB = 2**20


def dense_block(tiles, ids, count, tile_rows, tile_cols):
    slots = jnp.arange(tiles.shape[0], dtype=jnp.int32)
    live = jnp.where((slots < count)[:, None, None], tiles, jnp.zeros_like(tiles))
    blank = jnp.zeros((tile_rows * tile_cols, 128, 128), tiles.dtype)
    placed = blank.at[ids].add(live, unique_indices=True)
    placed = placed.reshape(tile_rows, tile_cols, 128, 128)
    return placed.transpose(0, 2, 1, 3).reshape(tile_rows * 128, tile_cols * 128)


def per_device_any(features, weight, bias, self_scale, adj_tiles, tile_ids, tile_counts, cotangent):
    row_block = self_scale.shape[0]
    col_block = features.shape[0]
    block = dense_block(
        adj_tiles[0, 0], tile_ids[0, 0], tile_counts[0, 0], row_block // 128, col_block // 128
    )
    start_row = lax.axis_index("row") * row_block
    col_no = lax.axis_index("col")
    inside = col_no == start_row // col_block
    offset = jnp.where(inside, start_row - col_no * col_block, 0)
    self_rows = jnp.where(inside, self_scale, 0.0)[:, None]
    piece = lax.all_gather(features, "row", axis=1, tiled=True)
    terms = jnp.dot(block, piece, preferred_element_type=F32)
    terms = terms + self_rows * lax.dynamic_slice_in_dim(piece, offset, row_block, 0)
    layer_in = lax.psum_scatter(terms, "col", scatter_dimension=0, tiled=True).astype(BF16)
    pre_act = jnp.dot(layer_in, weight, preferred_element_type=F32) + bias.astype(F32)
    sig = jax.nn.sigmoid(pre_act)
    outputs = pre_act * sig
    slope = sig * (1.0 + pre_act * (1.0 - sig))
    d_pre = (cotangent.astype(F32) * slope).astype(BF16)
    d_weight = lax.dot_general(
        layer_in, d_pre, (((0,), (0,)), ((), ())), preferred_element_type=F32
    )
    d_bias = jnp.sum(d_pre.astype(F32), axis=0)
    d_weight, d_bias = lax.psum((d_weight, d_bias), ("row", "col"))
    d_layer = lax.dot_general(
        d_pre, weight, (((1,), (1,)), ((), ())), preferred_element_type=F32
    ).astype(BF16)
    whole = lax.all_gather(d_layer, "col", axis=0, tiled=True)
    spread = lax.dot_general(block, whole, (((0,), (0,)), ((), ())), preferred_element_type=F32)
    own = lax.dynamic_slice_in_dim(spread, offset, row_block, 0) + self_rows * whole
    spread = lax.dynamic_update_slice_in_dim(spread, own, offset, 0)
    d_features = lax.psum_scatter(spread, "row", scatter_dimension=1, tiled=True)
    return outputs, d_features, d_weight, d_bias


def fused_kernel(
    slot_ref, live_ref, tiles_ref, feat_ref, w_ref, bias_ref, scale_ref, cot_ref,
    out_ref, dfeat_ref, dw_ref, db_ref,
    adj, hid, wv, sbuf, scol, xs, xr, keep, lay, xrow, pre, pt, ptg, dls, dlq,
    dwf, dwp, dwr, fw, dff, dfp, agg, fin, bsum, ssem, rsem, lsem,
):
    r = lax.axis_index("row")
    x = lax.axis_index("col")
    z = r // 4
    y = (r // 2) % 2
    k = r % 2
    q = 2 * y + k
    ends = (z == 0) | (z == 3)
    mids = (z == 1) | (z == 2)

    def at(xx, yy, zz, kk):
        return (zz * 4 + yy * 2 + kk, xx)

    sib = at(x, y, z, 1 - k)
    xn = at(1 - x, y, z, k)
    yn = at(x, 1 - y, z, k)
    dg = at(x, 1 - y, z, 1 - k)
    zr = at(x, y, jnp.minimum(z + 1, 3), k)
    zl = at(x, y, jnp.maximum(z - 1, 0), k)
    q_y = 2 * (1 - y) + k
    q_s = 2 * y + 1 - k
    q_d = 3 - q

    count = [0]
    sent = []

    def new():
        count[0] += 1
        return count[0] - 1

    def when(cond, fn):
        if cond is None:
            fn()
        else:
            pl.when(cond)(fn)

    def copy(i, src, dst, to):
        return pltpu.make_async_remote_copy(
            src_ref=src, dst_ref=dst, send_sem=ssem.at[i], recv_sem=rsem.at[i],
            device_id=to, device_id_type=MESH,
        )

    def send(i, src, dst, to, cond=None):
        c = copy(i, src, dst, to)
        when(cond, c.start)
        sent.append((c, cond))

    def recv(i, dst, cond=None):
        c = copy(i, dst, dst, sib)
        when(cond, c.wait_recv)

    def slice_at(o):
        return [z, z + 1 - 2 * (z % 2), 2 - z // 2, 3 - 3 * (z // 2)][o]

    def mult(v, n):
        return pl.multiple_of(v, n)

    barrier = pltpu.get_barrier_semaphore()
    peers = [at(xx, yy, z, kk) for xx, yy, kk in (
        (x, y, 1 - k), (x, 1 - y, k), (x, 1 - y, 1 - k), (1 - x, y, k),
        (1 - x, y, 1 - k), (1 - x, 1 - y, k), (1 - x, 1 - y, 1 - k))]
    peers += [at(x, y, (z + d) % 4, k) for d in (1, 2, 3)]
    for peer in peers:
        pl.semaphore_signal(barrier, inc=1, device_id=peer, device_id_type=MESH)

    w_copy = pltpu.make_async_copy(w_ref, wv, lsem.at[0])
    h_copy = pltpu.make_async_copy(feat_ref, hid.at[z], lsem.at[1])
    h_copy.start()

    for c in range(2):
        @pl.loop(0, 16)
        def _(t, c=c):
            p = c * 16 + t
            tile = tiles_ref[slot_ref[p]].astype(F32) * live_ref[p]
            adj[pl.ds(mult(c * 512 + q * 128, 128), 128), pl.ds(mult(t * 128, 128), 128)] = (
                tile.astype(BF16)
            )
    for i in range(4):
        sbuf[q, 2 * i:2 * i + 2, :] = scale_ref[...]
    h_copy.wait()
    w_copy.start()
    pl.semaphore_wait(barrier, len(peers))

    def h_part(s, c):
        return hid.at[s, pl.ds(c * 1024, 1024)]

    right = {(d, c): new() for d in (1, 2, 3) for c in (0, 1)}
    left = {(d, c): new() for d in (1, 2, 3) for c in (0, 1)}

    def line_send(ids, part, d, c, own_ok=True):
        sr, sl = jnp.maximum(z - (d - 1), 0), jnp.minimum(z + d - 1, 3)
        send(ids[0][d, c], part(sr, c), part(sr, c), zr, (z >= d - 1) & (z <= 2))
        send(ids[1][d, c], part(sl, c), part(sl, c), zl, (z <= 4 - d) & (z >= 1))

    def line_recv(ids, part, d, c):
        sr, sl = jnp.maximum(z - d, 0), jnp.minimum(z + d, 3)
        recv(ids[0][d, c], part(sr, c), z >= d)
        recv(ids[1][d, c], part(sl, c), z <= 3 - d)

    hz = (right, left)
    line_send(hz, h_part, 1, 0)
    line_send(hz, h_part, 1, 1)

    s_id = [new() for _ in range(3)]
    for i, to in zip(s_id, (yn, sib, dg)):
        send(i, sbuf.at[q], sbuf.at[q], to)

    def a_part(qq, c):
        return adj.at[pl.ds(mult(c * 512 + qq * 128, 128), 128)]

    ay = [new() for _ in range(2)]
    asib = [new() for _ in range(2)]
    afwd = [new() for _ in range(2)]
    for c in range(2):
        send(ay[c], a_part(q, c), a_part(q, c), yn)
    for c in range(2):
        send(asib[c], a_part(q, c), a_part(q, c), sib)

    line_recv(hz, h_part, 1, 0)
    line_send(hz, h_part, 2, 0)
    line_recv(hz, h_part, 1, 1)
    line_send(hz, h_part, 2, 1)
    recv(ay[0], a_part(q_y, 0))
    send(afwd[0], a_part(q_y, 0), a_part(q_y, 0), sib)

    for i, qq in zip(s_id, (q_y, q_s, q_d)):
        recv(i, sbuf.at[qq])
    inside = jnp.where(x == z // 2, 1.0, 0.0)
    for b in range(8):
        row = sbuf[b % 4, b // 4:b // 4 + 1, :] * inside
        scol[b] = jnp.broadcast_to(row, (128, 128)).T

    line_recv(hz, h_part, 2, 0)
    line_send(hz, h_part, 3, 0)
    line_recv(hz, h_part, 2, 1)
    line_send(hz, h_part, 3, 1)
    recv(ay[1], a_part(q_y, 1))
    send(afwd[1], a_part(q_y, 1), a_part(q_y, 1), sib)
    for c in range(2):
        recv(asib[c], a_part(q_s, c))
    for c in range(2):
        recv(afwd[c], a_part(q_d, c))

    x_id = [new() for _ in range(4)]
    l_id = [new() for _ in range(4)]
    row_id = [[new() for _ in range(3)] for _ in range(4)]
    w_waited = []

    def aggregate(o):
        s = slice_at(o)
        for c, sending in ((1 - x, True), (x, False)):
            acc = jnp.dot(
                adj[pl.ds(mult(c * 512, 512), 512), :], hid[s], preferred_element_type=F32
            )
            own = []
            for qq in range(4):
                first = mult((z % 2) * 1024 + qq * 256 + c * 128, 128)
                own.append(scol[c * 4 + qq] * hid[s, pl.ds(first, 128), :].astype(F32))
            acc = acc + jnp.concatenate(own, axis=0)
            if sending:
                xs[o] = acc.astype(BF16)
                send(x_id[o], xs.at[o], xr.at[o], xn)
            else:
                keep[o] = acc

    def combine(o):
        s = slice_at(o)
        recv(x_id[o], xr.at[o])
        mine = pl.ds(mult(x * 512, 512), 512)
        lay[s, mine, :] = (keep[o] + xr[o].astype(F32)).astype(BF16)
        for i, qq, to in zip(row_id[o], (q_y, q_d, q_s), (yn, dg, sib)):
            rows = pl.ds(mult(x * 512 + qq * 128, 128), 128)
            send(i, lay.at[s, rows], xrow.at[s * 4 + q], to)
        send(l_id[o], lay.at[s, mine], lay.at[s, mine], xn)
        xrow[s * 4 + q] = lay[s, pl.ds(mult(x * 512 + q * 128, 128), 128), :]

    def linear(o):
        s = slice_at(o)
        for i, qq in zip(row_id[o], (q_y, q_d, q_s)):
            recv(i, xrow.at[s * 4 + qq])
        if not w_waited:
            w_copy.wait()
            w_waited.append(True)
        part = jnp.concatenate([xrow[s * 4 + i] for i in range(4)], axis=1)

        @pl.loop(0, 4)
        def _(t):
            cols = pl.ds(mult(t * 512, 512), 512)
            prod = jnp.dot(
                part, wv[pl.ds(mult(s * 512, 512), 512), cols], preferred_element_type=F32
            )
            if o == 0:
                pre[:, cols] = prod + bias_ref[:, cols]
            else:
                pre[:, cols] += prod

    aggregate(0)
    aggregate(1)
    combine(0)
    aggregate(2)
    combine(1)
    linear(0)
    combine(2)
    linear(1)
    line_recv(hz, h_part, 3, 0)
    line_recv(hz, h_part, 3, 1)
    aggregate(3)
    linear(2)
    combine(3)
    linear(3)

    @pl.loop(0, 16)
    def _(t):
        cols = pl.ds(mult(t * 128, 128), 128)
        v = pre[:, cols]
        sig = jax.nn.sigmoid(v)
        out_ref[:, cols] = v * sig
        slope = sig * (1.0 + v * (1.0 - sig))
        d = (cot_ref[:, cols].astype(F32) * slope).astype(BF16)
        d32 = d.astype(F32)
        pt[pl.ds(mult(t * 128, 128), 128), :] = d32.T.astype(BF16)
        bsum[0, pl.ds(t, 1), :] = jnp.sum(d32, axis=0, keepdims=True)

    def p_half(c):
        return pt.at[pl.ds(mult(c * 1024, 1024), 1024)]

    b_own, b_x = x * 4 + q, (1 - x) * 4 + q
    px, py, pyf, ps, psf, pd, pdf = (new() for _ in range(7))
    send(px, p_half(1 - x), ptg.at[b_own], xn)
    send(py, p_half(x), ptg.at[b_own], yn)
    send(ps, p_half(x), ptg.at[b_own], sib)
    b_ids = [new() for _ in range(6)]
    send(b_ids[0], bsum.at[0], bsum.at[1], xn)
    ptg[b_own] = pt[pl.ds(mult(x * 1024, 1024), 1024), :]

    dl_ids = [new() for _ in range(7)]
    dl_to = [
        (x, 1 - y, k), (x, 1 - y, 1 - k), (x, y, 1 - k),
        (1 - x, y, k), (1 - x, y, 1 - k), (1 - x, 1 - y, k), (1 - x, 1 - y, 1 - k),
    ]

    @pl.loop(0, 4)
    def _(s):
        acc = jnp.dot(
            wv[pl.ds(mult(s * 512, 512), 512), :], pt[...], preferred_element_type=F32
        ).astype(BF16)
        for qq in range(4):
            dls[qq, s] = acc[qq * 128:(qq + 1) * 128]

    recv(px, ptg.at[b_x])
    send(pyf, ptg.at[b_x], ptg.at[b_x], yn)
    for i, (xx, yy, kk) in zip(dl_ids, dl_to):
        send(i, dls.at[2 * yy + kk], dlq.at[b_own], at(xx, yy, z, kk))
    send(psf, ptg.at[b_x], ptg.at[b_x], sib)
    recv(b_ids[0], bsum.at[1])
    bsum[2] = bsum[0] + bsum[1]
    send(b_ids[1], bsum.at[2], bsum.at[3], yn)
    dlq[b_own] = dls[q]
    recv(py, ptg.at[x * 4 + q_y])
    send(pd, ptg.at[x * 4 + q_y], ptg.at[x * 4 + q_y], sib)
    recv(b_ids[1], bsum.at[3])
    bsum[4] = bsum[2] + bsum[3]
    send(b_ids[2], bsum.at[4], bsum.at[5], sib)
    recv(pyf, ptg.at[(1 - x) * 4 + q_y])
    send(pdf, ptg.at[(1 - x) * 4 + q_y], ptg.at[(1 - x) * 4 + q_y], sib)
    recv(ps, ptg.at[x * 4 + q_s])
    recv(psf, ptg.at[(1 - x) * 4 + q_s])
    recv(pd, ptg.at[x * 4 + q_d])
    recv(pdf, ptg.at[(1 - x) * 4 + q_d])
    for o in range(4):
        recv(l_id[o], lay.at[slice_at(o), pl.ds(mult((1 - x) * 512, 512), 512)])

    dw_ids = [[new() for _ in range(3)] for _ in range(2)]
    for h in range(2):
        rows = pl.ds(h * 512, 512)
        lhs = jnp.concatenate([ptg[b, rows, :] for b in range(8)], axis=1)
        rhs = jnp.concatenate([lay[s] for s in range(4)], axis=1)
        acc = jnp.dot(lhs, rhs, preferred_element_type=F32)
        for s in range(4):
            dwf[s, rows, :] = acc[:, s * 128:(s + 1) * 128]
            dwp[s, rows, :] = acc[:, s * 128:(s + 1) * 128].astype(BF16)
        for d in (2, 1, 3):
            to = (z + d) % 4
            send(dw_ids[h][d - 1], dwp.at[to, rows], dwr.at[z, rows], at(x, y, to, k))
    recv(b_ids[2], bsum.at[5])
    bsum[6] = bsum[4] + bsum[5]
    for d in (1, 2, 3):
        send(b_ids[2 + d], bsum.at[6], bsum.at[6 + d], at(x, y, (z + d) % 4, k))

    for i, (xx, yy, kk) in zip(dl_ids, dl_to):
        recv(i, dlq.at[xx * 4 + 2 * yy + kk])

    pair = z // 2
    e, m = 3 * pair, 1 + pair
    e2, m2 = 3 - 3 * pair, 2 - pair
    f_ids = [new() for _ in range(6)]

    def input_grad(first):
        lhs = jnp.concatenate(
            [dlq[b, pl.ds(first, 2)].reshape(256, 128) for b in range(8)], axis=1
        )

        @pl.loop(0, 8)
        def _(t):
            cols = pl.ds(mult(t * 256, 256), 256)
            acc = jnp.dot(lhs, adj[:, cols], preferred_element_type=F32)
            qq = t % 4
            own = jnp.where((x == z // 2) & (t // 4 == z % 2), 1.0, 0.0)
            diag = []
            for c in range(2):
                row = sbuf[qq, c:c + 1, :] * own
                diag.append(dlq[c * 4 + qq, pl.ds(first, 2)].reshape(256, 128).astype(F32) * row)
            acc = acc + jnp.concatenate(diag, axis=1)
            for i in range(2):
                dff[first + i, :, cols] = acc[i * 128:(i + 1) * 128]
                dfp[first + i, :, cols] = acc[i * 128:(i + 1) * 128].astype(BF16)

    mid_dev, end_dev = at(x, y, m, k), at(x, y, e, k)
    input_grad(2 * (1 - pair))
    send(f_ids[0], dfp.at[m2], agg.at[0], mid_dev, ends)
    send(f_ids[1], dfp.at[e2], agg.at[1], mid_dev, ends)
    input_grad(2 * pair)
    send(f_ids[2], dfp.at[m], fin.at[0], mid_dev, ends)
    send(f_ids[3], dfp.at[e], fin.at[0], end_dev, mids)

    for h in range(2):
        rows = pl.ds(h * 512, 512)
        for d in (1, 2, 3):
            recv(dw_ids[h][d - 1], dwr.at[(z - d) % 4, rows])
        for t in range(4):
            rr = pl.ds(h * 512 + t * 128, 128)
            tot = dwf[z, rr, :]
            for d in (1, 2, 3):
                tot = tot + dwr[(z + d) % 4, rr, :].astype(F32)
            fw[:, rr] = tot.T.astype(BF16)
    for d in (1, 2, 3):
        recv(b_ids[2 + d], bsum.at[6 + d])
    db_ref[...] = bsum[6] + bsum[7] + bsum[8] + bsum[9]

    def piece(s, qq, c, first=0, rows=128):
        return dw_ref.at[
            pl.ds(mult(s * 512 + qq * 128 + first, 64), rows), pl.ds(mult(c * 1024, 1024), 1024)
        ]

    own_copy = pltpu.make_async_copy(fw, piece(z, q, x), lsem.at[2])
    own_copy.start()
    gz = ({(d, 0): new() for d in (1, 2, 3)}, {(d, 0): new() for d in (1, 2, 3)})
    gx, gy, gs, gxy, gyx, gsx, gsy, gsd1, gsd2 = (
        [new() for _ in range(4)] for _ in range(9)
    )

    def z_piece(s, c):
        return piece(s, q, x)

    send(gz[0][1, 0], fw, piece(z, q, x), zr, z <= 2)
    send(gz[1][1, 0], fw, piece(z, q, x), zl, z >= 1)

    def spread(o):
        s = slice_at(o)
        src = fw if o == 0 else piece(s, q, x)
        send(gx[o], src, piece(s, q, x), xn)
        send(gy[o], src, piece(s, q, x), yn)
        send(gs[o], src, piece(s, q, x), sib)

    def relay(o):
        s = slice_at(o)
        from_x, from_y = piece(s, q, 1 - x), piece(s, q_y, x)
        recv(gx[o], from_x)
        top = piece(s, q, 1 - x, 0, 64)
        send(gxy[o], top, top, yn)
        send(gsx[o], from_x, from_x, sib)
        recv(gy[o], from_y)
        low = piece(s, q_y, x, 64, 64)
        send(gyx[o], low, low, xn)
        send(gsy[o], from_y, from_y, sib)

    def relay_diag(o):
        s = slice_at(o)
        top = piece(s, q_y, 1 - x, 0, 64)
        recv(gxy[o], top)
        send(gsd1[o], top, top, sib)
        low = piece(s, q_y, 1 - x, 64, 64)
        recv(gyx[o], low)
        send(gsd2[o], low, low, sib)

    def last(o):
        s = slice_at(o)
        recv(gs[o], piece(s, q_s, x))
        recv(gsx[o], piece(s, q_s, 1 - x))
        recv(gsy[o], piece(s, q_d, x))
        recv(gsd1[o], piece(s, q_d, 1 - x, 0, 64))
        recv(gsd2[o], piece(s, q_d, 1 - x, 64, 64))

    spread(0)

    for j, (s_to, to) in enumerate(((m2, at(x, y, m2, k)), (e2, at(x, y, e2, k)))):
        recv(f_ids[j], agg.at[j], mids)

        @pl.when(mids)
        def _(j=j, s_to=s_to):
            dfp[s_to] = (dff[s_to] + agg[j].astype(F32)).astype(BF16)
        send(f_ids[4 + j], dfp.at[s_to], fin.at[1], to, mids)

    line_recv(gz, z_piece, 1, 0)
    line_send(gz, z_piece, 2, 0)
    spread(1)
    relay(0)
    line_recv(gz, z_piece, 2, 0)
    line_send(gz, z_piece, 3, 0)
    spread(2)
    relay(1)
    relay_diag(0)
    line_recv(gz, z_piece, 3, 0)
    spread(3)
    relay(2)
    relay_diag(1)

    recv(f_ids[2], fin.at[0], mids)
    recv(f_ids[3], fin.at[0], ends)
    recv(f_ids[4], fin.at[1], mids)
    recv(f_ids[5], fin.at[1], ends)

    @pl.loop(0, 16)
    def _(t):
        cols = pl.ds(mult(t * 128, 128), 128)
        tot = dff[z, :, cols] + fin[0, :, cols].astype(F32) + fin[1, :, cols].astype(F32)
        dfeat_ref[pl.ds(mult(t * 128, 128), 128), :] = tot.T

    relay(3)
    relay_diag(2)
    relay_diag(3)
    for o in range(4):
        last(o)
    own_copy.wait()
    for c, cond in sent:
        when(cond, c.wait_send)


N_SEMS = 140


def per_device_fused(features, weight, bias, self_scale, adj_tiles, tile_ids, tile_counts, cotangent):
    ids = tile_ids[0, 0]
    slots = jnp.arange(32, dtype=jnp.int32)
    hit = ids[None, :] == slots[:, None]
    slot_of = jnp.sum(jnp.where(hit, slots[None, :], 0), axis=1)
    live = (slot_of < tile_counts[0, 0]).astype(F32)
    vmem = pl.BlockSpec(memory_space=pltpu.VMEM)
    smem = pl.BlockSpec(memory_space=pltpu.SMEM)
    hbm = pl.BlockSpec(memory_space=pl.ANY)
    outputs, d_features, d_weight, d_bias = pl.pallas_call(
        fused_kernel,
        out_shape=(
            jax.ShapeDtypeStruct((128, 2048), F32),
            jax.ShapeDtypeStruct((2048, 128), F32),
            jax.ShapeDtypeStruct((2048, 2048), BF16),
            jax.ShapeDtypeStruct((16, 128), F32),
        ),
        in_specs=[smem, smem, vmem, hbm, hbm, vmem, vmem, vmem],
        out_specs=(vmem, vmem, hbm, vmem),
        scratch_shapes=[
            pltpu.VMEM((1024, 2048), BF16),
            pltpu.VMEM((4, 2048, 128), BF16),
            pltpu.VMEM((2048, 2048), BF16),
            pltpu.VMEM((4, 8, 128), F32),
            pltpu.VMEM((8, 128, 128), F32),
            pltpu.VMEM((4, 512, 128), BF16),
            pltpu.VMEM((4, 512, 128), BF16),
            pltpu.VMEM((4, 512, 128), F32),
            pltpu.VMEM((4, 1024, 128), BF16),
            pltpu.VMEM((16, 128, 128), BF16),
            pltpu.VMEM((128, 2048), F32),
            pltpu.VMEM((2048, 128), BF16),
            pltpu.VMEM((8, 1024, 128), BF16),
            pltpu.VMEM((4, 4, 128, 128), BF16),
            pltpu.VMEM((8, 4, 128, 128), BF16),
            pltpu.VMEM((4, 1024, 128), F32),
            pltpu.VMEM((4, 1024, 128), BF16),
            pltpu.VMEM((4, 1024, 128), BF16),
            pltpu.VMEM((128, 1024), BF16),
            pltpu.VMEM((4, 128, 2048), F32),
            pltpu.VMEM((4, 128, 2048), BF16),
            pltpu.VMEM((2, 128, 2048), BF16),
            pltpu.VMEM((2, 128, 2048), BF16),
            pltpu.VMEM((10, 16, 128), F32),
            pltpu.SemaphoreType.DMA((N_SEMS,)),
            pltpu.SemaphoreType.DMA((N_SEMS,)),
            pltpu.SemaphoreType.DMA((3,)),
        ],
        compiler_params=pltpu.CompilerParams(
            collective_id=0, has_side_effects=True, vmem_limit_bytes=62 * MIB
        ),
        cost_estimate=pl.CostEstimate(
            flops=7_600_000_000, bytes_accessed=24 * MIB, transcendentals=262144
        ),
    )(
        slot_of, live, adj_tiles[0, 0], features, weight,
        bias.astype(F32).reshape(1, 2048), self_scale.reshape(2, 128), cotangent,
    )
    return outputs, d_features, d_weight.astype(F32), d_bias.reshape(2048)


def solution(mesh):
    fits = dict(mesh.shape) == {"row": 16, "col": 2}

    def run(*arrays):
        fused = fits and arrays[0].shape == (4096, 2048) and arrays[4].shape[2] == 32
        return jax.shard_map(
            per_device_fused if fused else per_device_any,
            mesh=mesh,
            in_specs=(
                P("col", "row"),
                P(),
                P(),
                P("row"),
                P("row", "col", None, None, None),
                P("row", "col", None),
                P("row", "col"),
                P(("row", "col"), None),
            ),
            out_specs=(P(("row", "col"), None), P("col", "row"), P(), P()),
            check_vma=False,
        )(*arrays)

    return run
```

time: 748 us -> 201 us (0.27)
  waiting for transfers between devices: 408 us -> 0 us
  Pallas kernels: 0 us -> 182 us
  local copies, waits for them, and re-layouts: 106 us -> 2.56 us
  other arithmetic: 116 us -> 14.4 us
  matrix products: 56.8 us -> 0 us
  blocking collectives: 40.8 us -> 0 us
  between operations: 14.6 us -> 1.32 us
    reduce_scatter x2 -> x0, waiting for transfers between devices: 214 us -> none  [the longest x1 182 us: per_device(): lax.psum_scatter(spread, 'row', scatter_dimension=1, tiled=True)]
    pallas_call x0 -> x1, Pallas kernels: none -> 182 us  [per_device_fused(): pl.pallas_call(fused_kernel, out_shape=(jax.ShapeDtypeStruct((128, 2048),...]
    scatter-add x2 -> x0, other arithmetic: 107 us -> none  [add_group(): return running.at[to_ids].add(products)]
    psum x1 -> x0, waiting for transfers between devices: 103 us -> none  [per_device(): d_weight, d_bias = lax.psum((d_weight_part, d_bias_part), ('row', 'col'))]
    all_gather x2 -> x0, waiting for transfers between devices: 89.7 us -> none  [the longest x1 77 us: per_device(): lax.all_gather(features, 'row', axis=1, tiled=True)]
    select_n x2 -> x0, local copies, waits for them, and re-layouts: 67.2 us -> none  [add_group(): products = jnp.where(live_slot[:, None, None], products, 0.0)]
    dot_general x5 -> x0, matrix products: 56.8 us -> none  [the longest x2 37.5 us: add_group(): jnp.einsum(pattern, tile_group, pieces, preferred_element_type=jnp.float32)]
    psum x1 -> x0, blocking collectives: 40.8 us -> none  [per_device(): d_weight, d_bias = lax.psum((d_weight_part, d_bias_part), ('row', 'col'))]
  transfers between devices with their start and end apart: 5 -> 0, of which waited for: 5 -> 0; matrix products, arithmetic and copies ran while one was open for 20% -> 0% of each run, Pallas kernels for 0% -> 0%
where the time goes in v1:
time: 201 us; the launch traced here: 200 us
  Pallas kernels  182 us (91%)
  other arithmetic  14.4 us (7%)
  local copies, waits for them, and re-layouts  2.56 us (1%)
    pallas_call x1, Pallas kernels, per_device_fused(): pl.pallas_call(fused_kernel, out_shape=(jax.ShapeDtypeStruct((128, 2048),...  182 us
    convert_element_type x1, other arithmetic, per_device_fused(): return (outputs, d_features, d_weight.astype(F32), d_bias.reshape(2048))  11.8 us

profile of v1, /device:TPU:8, one launch (start us, length us, event | category | flops | bytes accessed | tf_op | source)
XLA Modules:
  0.0 200.0 jit_solution(6611761639969290898)
XLA Ops:
  1.3 0.8 select_reduce_fusion.slot_ref
  2.0 0.0 copy-start.3
  2.1 0.5 compare_convert_fusion.live_ref
  2.6 1.3 reshape.24
  3.9 0.0 copy-done.3
  3.9 181.8 %shard_map.111 = (f32[128,2048]{1,0:T(8,128)}, f32[2048,128]{1,0:T(8,128)}, bf16[2048,2048]{1,0:T(8,128)(2,1)}, f32[16,128]{1,0:T(8,128)}) custom-call(s32[32]{0:T(128)} %copy-done.3, f32[32]{0:T(128)} %compare_convert_fusion.live_ref, bf16[32,128,128]{2,1,0:T(8,128)(2,1)} %bitcast.9, bf16[2048,128]{1,0:T(8,128)(2,1)} %feat_ref.1, bf16[2048,2048]{1,0:T(8,128)(2,1)} %w_ref.1, ...), custom_call_target="tpu_custom_call" | custom-call | flops 7600000000 | bytes 25165824 | tf_op jit(solution)/shard_map/pallas_call | solution.py:514
  185.6 0.0 copy-start.1
  185.6 0.0 copy-start
  185.7 0.0 copy-start.2
  185.7 11.8 %convert_element_type.8 = f32[2048,2048]{1,0:T(8,128)} convert(bf16[2048,2048]{1,0:T(8,128)(2,1)} %get-tuple-element.10) | non-fusion elementwise | flops 4194304 | bytes 25165824 | tf_op jit(solution)/shard_map/convert_element_type | solution.py:563
  197.5 0.0 copy-done.1
  197.5 1.0 copy.16
  198.5 0.0 copy-done
  198.5 1.0 copy.17
  199.4 0.0 copy-done.2
  199.4 0.6 copy.18
Async XLA Ops:
  2.0 1.8 copy-start.3
  185.6 11.8 %copy-start.1 = (f32[128,2048]{1,0:T(8,128)S(1)}, f32[128,2048]{1,0:T(8,128)}, u32[]{:S(2)}) copy-start(f32[128,2048]{1,0:T(8,128)} %get-tuple-element.16) | copy-start | bytes 3145732
  185.6 12.8 %copy-start = (f32[2048,128]{1,0:T(8,128)S(1)}, f32[2048,128]{1,0:T(8,128)}, u32[]{:S(2)}) copy-start(f32[2048,128]{1,0:T(8,128)} %get-tuple-element.17) | copy-start | bytes 3145732
  185.7 13.8 %copy-start.2 = (f32[16,128]{1,0:T(8,128)S(1)}, f32[16,128]{1,0:T(8,128)}, u32[]{:S(2)}) copy-start(f32[16,128]{1,0:T(8,128)} %get-tuple-element.11) | copy-start | bytes 24580

commit v2 on v1

--- a/solution.py
+++ b/solution.py
@@ -57,10 +57,10 @@
 
 
 def fused_kernel(
-    slot_ref, live_ref, tiles_ref, feat_ref, w_ref, bias_ref, scale_ref, cot_ref,
+    ids_ref, count_ref, tiles_ref, feat_ref, w_ref, bias_ref, scale_ref, cot_ref,
     out_ref, dfeat_ref, dw_ref, db_ref,
     adj, hid, wv, sbuf, scol, xs, xr, keep, lay, xrow, pre, pt, ptg, dls, dlq,
-    dwf, dwp, dwr, fw, dff, dfp, agg, fin, bsum, ssem, rsem, lsem,
+    dwf, dwp, dwr, dff, dfp, agg, fin, bsum, ssem, rsem, lsem,
 ):
     r = lax.axis_index("row")
     x = lax.axis_index("col")
@@ -85,7 +85,8 @@
     q_d = 3 - q
 
     count = [0]
-    sent = []
+    sent_by = {}
+    pending = {}
 
     def new():
         count[0] += 1
@@ -103,12 +104,14 @@
             device_id=to, device_id_type=MESH,
         )
 
-    def send(i, src, dst, to, cond=None):
+    def send(i, src, dst, to, cond=None, rcond=None):
         c = copy(i, src, dst, to)
         when(cond, c.start)
-        sent.append((c, cond))
+        sent_by[i] = (c, cond)
+        pending[i] = (dst, rcond)
 
     def recv(i, dst, cond=None):
+        pending.pop(i)
         c = copy(i, dst, dst, sib)
         when(cond, c.wait_recv)
 
@@ -133,8 +136,11 @@
     for c in range(2):
         @pl.loop(0, 16)
         def _(t, c=c):
-            p = c * 16 + t
-            tile = tiles_ref[slot_ref[p]].astype(F32) * live_ref[p]
+            slot = jnp.int32(0)
+            for i in range(32):
+                slot = jnp.where(ids_ref[i] == c * 16 + t, i, slot)
+            live = jnp.where(slot < count_ref[0], 1.0, 0.0)
+            tile = tiles_ref[slot].astype(F32) * live
             adj[pl.ds(mult(c * 512 + q * 128, 128), 128), pl.ds(mult(t * 128, 128), 128)] = (
                 tile.astype(BF16)
             )
@@ -152,8 +158,8 @@
 
     def line_send(ids, part, d, c, own_ok=True):
         sr, sl = jnp.maximum(z - (d - 1), 0), jnp.minimum(z + d - 1, 3)
-        send(ids[0][d, c], part(sr, c), part(sr, c), zr, (z >= d - 1) & (z <= 2))
-        send(ids[1][d, c], part(sl, c), part(sl, c), zl, (z <= 4 - d) & (z >= 1))
+        send(ids[0][d, c], part(sr, c), part(sr, c), zr, (z >= d - 1) & (z <= 2), z >= d)
+        send(ids[1][d, c], part(sl, c), part(sl, c), zl, (z <= 4 - d) & (z >= 1), z <= 3 - d)
 
     def line_recv(ids, part, d, c):
         sr, sl = jnp.maximum(z - d, 0), jnp.minimum(z + d, 3)
@@ -272,48 +278,57 @@
     combine(3)
     linear(3)
 
-    @pl.loop(0, 16)
-    def _(t):
-        cols = pl.ds(mult(t * 128, 128), 128)
-        v = pre[:, cols]
-        sig = jax.nn.sigmoid(v)
-        out_ref[:, cols] = v * sig
-        slope = sig * (1.0 + v * (1.0 - sig))
-        d = (cot_ref[:, cols].astype(F32) * slope).astype(BF16)
-        d32 = d.astype(F32)
-        pt[pl.ds(mult(t * 128, 128), 128), :] = d32.T.astype(BF16)
-        bsum[0, pl.ds(t, 1), :] = jnp.sum(d32, axis=0, keepdims=True)
-
     def p_half(c):
         return pt.at[pl.ds(mult(c * 1024, 1024), 1024)]
 
+    def activate(c):
+        @pl.loop(0, 8)
+        def _(i):
+            t = c * 8 + i
+            cols = pl.ds(mult(t * 128, 128), 128)
+            v = pre[:, cols]
+            sig = jax.nn.sigmoid(v)
+            out_ref[:, cols] = v * sig
+            slope = sig * (1.0 + v * (1.0 - sig))
+            d32 = (cot_ref[:, cols].astype(F32) * slope).astype(BF16).astype(F32)
+            pt[pl.ds(mult(t * 128, 128), 128), :] = d32.T.astype(BF16)
+            bsum[0, pl.ds(t, 1), :] = jnp.sum(d32, axis=0, keepdims=True)
+
     b_own, b_x = x * 4 + q, (1 - x) * 4 + q
     px, py, pyf, ps, psf, pd, pdf = (new() for _ in range(7))
+    b_ids = [new() for _ in range(6)]
+    activate(1 - x)
     send(px, p_half(1 - x), ptg.at[b_own], xn)
+    activate(x)
     send(py, p_half(x), ptg.at[b_own], yn)
     send(ps, p_half(x), ptg.at[b_own], sib)
-    b_ids = [new() for _ in range(6)]
     send(b_ids[0], bsum.at[0], bsum.at[1], xn)
     ptg[b_own] = pt[pl.ds(mult(x * 1024, 1024), 1024), :]
 
-    dl_ids = [new() for _ in range(7)]
+    @pl.loop(0, 2)
+    def _(i):
+        acc = jnp.dot(
+            wv[pl.ds(mult(i * 1024, 1024), 1024), :], pt[...], preferred_element_type=F32
+        ).astype(BF16)
+        for j in range(2):
+            for qq in range(4):
+                first = j * 512 + qq * 128
+                dls[qq, i * 2 + j] = acc[first:first + 128]
+
     dl_to = [
-        (x, 1 - y, k), (x, 1 - y, 1 - k), (x, y, 1 - k),
-        (1 - x, y, k), (1 - x, y, 1 - k), (1 - x, 1 - y, k), (1 - x, 1 - y, 1 - k),
+        (1 - x, y, k), (1 - x, y, 1 - k), (x, y, 1 - k),
+        (x, 1 - y, k), (x, 1 - y, 1 - k), (1 - x, 1 - y, k), (1 - x, 1 - y, 1 - k),
     ]
-
-    @pl.loop(0, 4)
-    def _(s):
-        acc = jnp.dot(
-            wv[pl.ds(mult(s * 512, 512), 512), :], pt[...], preferred_element_type=F32
-        ).astype(BF16)
-        for qq in range(4):
-            dls[qq, s] = acc[qq * 128:(qq + 1) * 128]
+    dl_ids = [new() for _ in dl_to]
+
+    def send_layer_grad(which):
+        for i in which:
+            xx, yy, kk = dl_to[i]
+            send(dl_ids[i], dls.at[2 * yy + kk], dlq.at[b_own], at(xx, yy, z, kk))
 
     recv(px, ptg.at[b_x])
     send(pyf, ptg.at[b_x], ptg.at[b_x], yn)
-    for i, (xx, yy, kk) in zip(dl_ids, dl_to):
-        send(i, dls.at[2 * yy + kk], dlq.at[b_own], at(xx, yy, z, kk))
+    send_layer_grad((0, 1, 2))
     send(psf, ptg.at[b_x], ptg.at[b_x], sib)
     recv(b_ids[0], bsum.at[1])
     bsum[2] = bsum[0] + bsum[1]
@@ -321,11 +336,12 @@
     dlq[b_own] = dls[q]
     recv(py, ptg.at[x * 4 + q_y])
     send(pd, ptg.at[x * 4 + q_y], ptg.at[x * 4 + q_y], sib)
+    recv(pyf, ptg.at[(1 - x) * 4 + q_y])
+    send(pdf, ptg.at[(1 - x) * 4 + q_y], ptg.at[(1 - x) * 4 + q_y], sib)
+    send_layer_grad((3, 4, 5, 6))
     recv(b_ids[1], bsum.at[3])
     bsum[4] = bsum[2] + bsum[3]
     send(b_ids[2], bsum.at[4], bsum.at[5], sib)
-    recv(pyf, ptg.at[(1 - x) * 4 + q_y])
-    send(pdf, ptg.at[(1 - x) * 4 + q_y], ptg.at[(1 - x) * 4 + q_y], sib)
     recv(ps, ptg.at[x * 4 + q_s])
     recv(psf, ptg.at[(1 - x) * 4 + q_s])
     recv(pd, ptg.at[x * 4 + q_d])
@@ -356,132 +372,167 @@
     pair = z // 2
     e, m = 3 * pair, 1 + pair
     e2, m2 = 3 - 3 * pair, 2 - pair
-    f_ids = [new() for _ in range(6)]
+    f_in = [[new() for _ in range(2)] for _ in range(2)]
+    f_out = [[new() for _ in range(2)] for _ in range(2)]
+    f_fin = [new() for _ in range(2)]
 
     def input_grad(first):
         lhs = jnp.concatenate(
             [dlq[b, pl.ds(first, 2)].reshape(256, 128) for b in range(8)], axis=1
         )
 
-        @pl.loop(0, 8)
+        @pl.loop(0, 4)
         def _(t):
-            cols = pl.ds(mult(t * 256, 256), 256)
+            cols = pl.ds(mult(t * 512, 512), 512)
             acc = jnp.dot(lhs, adj[:, cols], preferred_element_type=F32)
-            qq = t % 4
-            own = jnp.where((x == z // 2) & (t // 4 == z % 2), 1.0, 0.0)
+            own = jnp.where((x == z // 2) & (t // 2 == z % 2), 1.0, 0.0)
             diag = []
-            for c in range(2):
-                row = sbuf[qq, c:c + 1, :] * own
-                diag.append(dlq[c * 4 + qq, pl.ds(first, 2)].reshape(256, 128).astype(F32) * row)
+            for j in range(2):
+                qq = (t % 2) * 2 + j
+                for c in range(2):
+                    row = sbuf[qq, c:c + 1, :] * own
+                    diag.append(dlq[c * 4 + qq, pl.ds(first, 2)].reshape(256, 128).astype(F32) * row)
             acc = acc + jnp.concatenate(diag, axis=1)
             for i in range(2):
                 dff[first + i, :, cols] = acc[i * 128:(i + 1) * 128]
                 dfp[first + i, :, cols] = acc[i * 128:(i + 1) * 128].astype(BF16)
 
     mid_dev, end_dev = at(x, y, m, k), at(x, y, e, k)
+    input_grad(2 * pair)
+    send(f_fin[0], dfp.at[e], fin.at[0], end_dev, mids, ends)
     input_grad(2 * (1 - pair))
-    send(f_ids[0], dfp.at[m2], agg.at[0], mid_dev, ends)
-    send(f_ids[1], dfp.at[e2], agg.at[1], mid_dev, ends)
-    input_grad(2 * pair)
-    send(f_ids[2], dfp.at[m], fin.at[0], mid_dev, ends)
-    send(f_ids[3], dfp.at[e], fin.at[0], end_dev, mids)
-
-    for h in range(2):
-        rows = pl.ds(h * 512, 512)
+
+    def cut(c):
+        return pl.ds(c * 1024, 1024)
+
+    def end_send(j, c):
+        s_to = (m2, e2)[j]
+        send(f_in[j][c], dfp.at[s_to, :, cut(c)], agg.at[j, :, cut(c)], mid_dev, ends, mids)
+
+    def end_wait(j, c):
+        out, cond = sent_by.pop(f_in[j][c])
+        pl.when(cond)(out.wait_send)
+
+    def mid_send(j, c):
+        s_to, to = ((m2, at(x, y, m2, k)), (e2, at(x, y, e2, k)))[j]
+        recv(f_in[j][c], agg.at[j, :, cut(c)], mids)
+
+        @pl.when(mids)
+        def _():
+            dfp[s_to, :, cut(c)] = (
+                dff[s_to, :, cut(c)] + agg[j, :, cut(c)].astype(F32)
+            ).astype(BF16)
+        send(f_out[j][c], dfp.at[s_to, :, cut(c)], fin.at[1, :, cut(c)], to, mids, (mids, ends)[j])
+
+    def piece(s, qq, c, h):
+        return dw_ref.at[(s * 4 + qq) * 4 + c * 2 + h]
+
+    gz = tuple({(d, h): new() for d in (1, 2, 3) for h in (0, 1)} for _ in range(2))
+    gx, gy, gs, gxy, gyx, gsx, gsy, gsd1, gsd2 = (
+        {(h, o): new() for h in (0, 1) for o in range(4)} for _ in range(9)
+    )
+
+    def z_piece(s, h):
+        return piece(s, q, x, h)
+
+    def finish(h):
         for d in (1, 2, 3):
-            recv(dw_ids[h][d - 1], dwr.at[(z - d) % 4, rows])
+            recv(dw_ids[h][d - 1], dwr.at[(z - d) % 4, pl.ds(h * 512, 512)])
         for t in range(4):
             rr = pl.ds(h * 512 + t * 128, 128)
             tot = dwf[z, rr, :]
             for d in (1, 2, 3):
                 tot = tot + dwr[(z + d) % 4, rr, :].astype(F32)
-            fw[:, rr] = tot.T.astype(BF16)
+            dw_ref[(z * 4 + q) * 4 + x * 2 + h, :, t * 128:(t + 1) * 128] = tot.T.astype(BF16)
+        line_send(gz, z_piece, 1, h)
+        spread(h, 0)
+
+    def spread(h, o):
+        src = piece(slice_at(o), q, x, h)
+        send(gx[h, o], src, src, xn)
+        send(gy[h, o], src, src, yn)
+        send(gs[h, o], src, src, sib)
+
+    def part(ref, i):
+        return ref.at[pl.ds(i * 64, 64)]
+
+    def relay(h, o):
+        s = slice_at(o)
+        from_x, from_y = piece(s, q, 1 - x, h), piece(s, q_y, x, h)
+        recv(gx[h, o], from_x)
+        send(gxy[h, o], part(from_x, 0), part(from_x, 0), yn)
+        send(gsx[h, o], from_x, from_x, sib)
+        recv(gy[h, o], from_y)
+        send(gyx[h, o], part(from_y, 1), part(from_y, 1), xn)
+        send(gsy[h, o], from_y, from_y, sib)
+
+    def relay_diag(h, o):
+        block = piece(slice_at(o), q_y, 1 - x, h)
+        recv(gxy[h, o], part(block, 0))
+        send(gsd1[h, o], part(block, 0), part(block, 0), sib)
+        recv(gyx[h, o], part(block, 1))
+        send(gsd2[h, o], part(block, 1), part(block, 1), sib)
+
+    def last(h, o):
+        s = slice_at(o)
+        recv(gs[h, o], piece(s, q_s, x, h))
+        recv(gsx[h, o], piece(s, q_s, 1 - x, h))
+        recv(gsy[h, o], piece(s, q_d, x, h))
+        block = piece(s, q_d, 1 - x, h)
+        recv(gsd1[h, o], part(block, 0))
+        recv(gsd2[h, o], part(block, 1))
+
+    def along(h, d):
+        line_recv(gz, z_piece, d, h)
+        if d < 3:
+            line_send(gz, z_piece, d + 1, h)
+        spread(h, d)
+
+    finish(0)
+    along(0, 1)
+    relay(0, 0)
+    finish(1)
+    end_send(0, 0)
+    end_send(0, 1)
+    along(0, 2)
+    relay(0, 1)
+    relay_diag(0, 0)
+    along(1, 1)
+    mid_send(0, 0)
+    end_wait(0, 0)
+    end_send(1, 0)
+    relay(1, 0)
+    relay_diag(0, 1)
+    along(0, 3)
+    mid_send(0, 1)
+    end_wait(0, 1)
+    end_send(1, 1)
+    relay(0, 2)
+    relay_diag(1, 0)
+    along(1, 2)
+    mid_send(1, 0)
+    end_wait(1, 0)
+    send(f_fin[1], dfp.at[m], fin.at[0], mid_dev, ends, mids)
+    relay(1, 1)
+    relay_diag(0, 2)
+    along(1, 3)
+    mid_send(1, 1)
+    relay(0, 3)
+    relay_diag(1, 1)
+    relay(1, 2)
+    relay_diag(0, 3)
+    relay(1, 3)
+    relay_diag(1, 2)
+    relay_diag(1, 3)
     for d in (1, 2, 3):
         recv(b_ids[2 + d], bsum.at[6 + d])
     db_ref[...] = bsum[6] + bsum[7] + bsum[8] + bsum[9]
 
-    def piece(s, qq, c, first=0, rows=128):
-        return dw_ref.at[
-            pl.ds(mult(s * 512 + qq * 128 + first, 64), rows), pl.ds(mult(c * 1024, 1024), 1024)
-        ]
-
-    own_copy = pltpu.make_async_copy(fw, piece(z, q, x), lsem.at[2])
-    own_copy.start()
-    gz = ({(d, 0): new() for d in (1, 2, 3)}, {(d, 0): new() for d in (1, 2, 3)})
-    gx, gy, gs, gxy, gyx, gsx, gsy, gsd1, gsd2 = (
-        [new() for _ in range(4)] for _ in range(9)
-    )
-
-    def z_piece(s, c):
-        return piece(s, q, x)
-
-    send(gz[0][1, 0], fw, piece(z, q, x), zr, z <= 2)
-    send(gz[1][1, 0], fw, piece(z, q, x), zl, z >= 1)
-
-    def spread(o):
-        s = slice_at(o)
-        src = fw if o == 0 else piece(s, q, x)
-        send(gx[o], src, piece(s, q, x), xn)
-        send(gy[o], src, piece(s, q, x), yn)
-        send(gs[o], src, piece(s, q, x), sib)
-
-    def relay(o):
-        s = slice_at(o)
-        from_x, from_y = piece(s, q, 1 - x), piece(s, q_y, x)
-        recv(gx[o], from_x)
-        top = piece(s, q, 1 - x, 0, 64)
-        send(gxy[o], top, top, yn)
-        send(gsx[o], from_x, from_x, sib)
-        recv(gy[o], from_y)
-        low = piece(s, q_y, x, 64, 64)
-        send(gyx[o], low, low, xn)
-        send(gsy[o], from_y, from_y, sib)
-
-    def relay_diag(o):
-        s = slice_at(o)
-        top = piece(s, q_y, 1 - x, 0, 64)
-        recv(gxy[o], top)
-        send(gsd1[o], top, top, sib)
-        low = piece(s, q_y, 1 - x, 64, 64)
-        recv(gyx[o], low)
-        send(gsd2[o], low, low, sib)
-
-    def last(o):
-        s = slice_at(o)
-        recv(gs[o], piece(s, q_s, x))
-        recv(gsx[o], piece(s, q_s, 1 - x))
-        recv(gsy[o], piece(s, q_d, x))
-        recv(gsd1[o], piece(s, q_d, 1 - x, 0, 64))
-        recv(gsd2[o], piece(s, q_d, 1 - x, 64, 64))
-
-    spread(0)
-
-    for j, (s_to, to) in enumerate(((m2, at(x, y, m2, k)), (e2, at(x, y, e2, k)))):
-        recv(f_ids[j], agg.at[j], mids)
-
-        @pl.when(mids)
-        def _(j=j, s_to=s_to):
-            dfp[s_to] = (dff[s_to] + agg[j].astype(F32)).astype(BF16)
-        send(f_ids[4 + j], dfp.at[s_to], fin.at[1], to, mids)
-
-    line_recv(gz, z_piece, 1, 0)
-    line_send(gz, z_piece, 2, 0)
-    spread(1)
-    relay(0)
-    line_recv(gz, z_piece, 2, 0)
-    line_send(gz, z_piece, 3, 0)
-    spread(2)
-    relay(1)
-    relay_diag(0)
-    line_recv(gz, z_piece, 3, 0)
-    spread(3)
-    relay(2)
-    relay_diag(1)
-
-    recv(f_ids[2], fin.at[0], mids)
-    recv(f_ids[3], fin.at[0], ends)
-    recv(f_ids[4], fin.at[1], mids)
-    recv(f_ids[5], fin.at[1], ends)
+    recv(f_fin[0], fin.at[0], ends)
+    recv(f_fin[1], fin.at[0], mids)
+    for c in range(2):
+        recv(f_out[0][c], fin.at[1, :, cut(c)], mids)
+        recv(f_out[1][c], fin.at[1, :, cut(c)], ends)
 
     @pl.loop(0, 16)
     def _(t):
@@ -489,38 +540,57 @@
         tot = dff[z, :, cols] + fin[0, :, cols].astype(F32) + fin[1, :, cols].astype(F32)
         dfeat_ref[pl.ds(mult(t * 128, 128), 128), :] = tot.T
 
-    relay(3)
-    relay_diag(2)
-    relay_diag(3)
-    for o in range(4):
-        last(o)
-    own_copy.wait()
-    for c, cond in sent:
+    for h in range(2):
+        for o in range(4):
+            last(h, o)
+    assert not pending
+    for i, (c, cond) in sent_by.items():
         when(cond, c.wait_send)
 
 
-N_SEMS = 140
+def widen_kernel(dw_ref, out_ref, dfeat_ref, db_ref, dw_out, out_out, dfeat_out, db_out, sem):
+    step = pl.program_id(0)
+    copies = [
+        pltpu.make_async_copy(src, dst, sem.at[i])
+        for i, (src, dst) in enumerate(
+            ((out_ref, out_out), (dfeat_ref, dfeat_out), (db_ref, db_out))
+        )
+    ]
+
+    @pl.when(step == 0)
+    def _():
+        for c in copies:
+            c.start()
+
+    for i in range(2):
+        for j in range(4):
+            dw_out[i * 128:(i + 1) * 128, j * 512:(j + 1) * 512] = (
+                dw_ref[(2 * step + i) * 4 + j].astype(F32)
+            )
+
+    @pl.when(step == pl.num_programs(0) - 1)
+    def _():
+        for c in copies:
+            c.wait()
+
+
+N_SEMS = 180
 
 
 def per_device_fused(features, weight, bias, self_scale, adj_tiles, tile_ids, tile_counts, cotangent):
-    ids = tile_ids[0, 0]
-    slots = jnp.arange(32, dtype=jnp.int32)
-    hit = ids[None, :] == slots[:, None]
-    slot_of = jnp.sum(jnp.where(hit, slots[None, :], 0), axis=1)
-    live = (slot_of < tile_counts[0, 0]).astype(F32)
     vmem = pl.BlockSpec(memory_space=pltpu.VMEM)
     smem = pl.BlockSpec(memory_space=pltpu.SMEM)
     hbm = pl.BlockSpec(memory_space=pl.ANY)
-    outputs, d_features, d_weight, d_bias = pl.pallas_call(
+    outputs, d_features, gathered, d_bias = pl.pallas_call(
         fused_kernel,
         out_shape=(
-            jax.ShapeDtypeStruct((128, 2048), F32),
-            jax.ShapeDtypeStruct((2048, 128), F32),
-            jax.ShapeDtypeStruct((2048, 2048), BF16),
-            jax.ShapeDtypeStruct((16, 128), F32),
+            pltpu.VMEM((128, 2048), F32),
+            pltpu.VMEM((2048, 128), F32),
+            pltpu.VMEM((64, 128, 512), BF16),
+            pltpu.VMEM((16, 128), F32),
         ),
         in_specs=[smem, smem, vmem, hbm, hbm, vmem, vmem, vmem],
-        out_specs=(vmem, vmem, hbm, vmem),
+        out_specs=(vmem, vmem, vmem, vmem),
         scratch_shapes=[
             pltpu.VMEM((1024, 2048), BF16),
             pltpu.VMEM((4, 2048, 128), BF16),
@@ -540,7 +610,6 @@
             pltpu.VMEM((4, 1024, 128), F32),
             pltpu.VMEM((4, 1024, 128), BF16),
             pltpu.VMEM((4, 1024, 128), BF16),
-            pltpu.VMEM((128, 1024), BF16),
             pltpu.VMEM((4, 128, 2048), F32),
             pltpu.VMEM((4, 128, 2048), BF16),
             pltpu.VMEM((2, 128, 2048), BF16),
@@ -551,16 +620,30 @@
             pltpu.SemaphoreType.DMA((3,)),
         ],
         compiler_params=pltpu.CompilerParams(
-            collective_id=0, has_side_effects=True, vmem_limit_bytes=62 * MIB
+            collective_id=0, has_side_effects=True, vmem_limit_bytes=50 * MIB
         ),
         cost_estimate=pl.CostEstimate(
             flops=7_600_000_000, bytes_accessed=24 * MIB, transcendentals=262144
         ),
     )(
-        slot_of, live, adj_tiles[0, 0], features, weight,
+        tile_ids[0, 0], tile_counts[0], adj_tiles[0, 0], features, weight,
         bias.astype(F32).reshape(1, 2048), self_scale.reshape(2, 128), cotangent,
     )
-    return outputs, d_features, d_weight.astype(F32), d_bias.reshape(2048)
+    d_weight, outputs, d_features, d_bias = pl.pallas_call(
+        widen_kernel,
+        grid=(8,),
+        out_shape=(
+            jax.ShapeDtypeStruct((2048, 2048), F32),
+            jax.ShapeDtypeStruct((128, 2048), F32),
+            jax.ShapeDtypeStruct((2048, 128), F32),
+            jax.ShapeDtypeStruct((16, 128), F32),
+        ),
+        in_specs=[vmem] * 4,
+        out_specs=(pl.BlockSpec((256, 2048), lambda i: (i, 0)), hbm, hbm, hbm),
+        scratch_shapes=[pltpu.SemaphoreType.DMA((3,))],
+        compiler_params=pltpu.CompilerParams(vmem_limit_bytes=20 * MIB),
+    )(gathered, outputs, d_features, d_bias)
+    return outputs, d_features, d_weight, d_bias.reshape(2048)
 
 
 def solution(mesh):

time: 201 us -> 164 us (0.82)
  Pallas kernels: 182 us -> 159 us
  other arithmetic: 14.4 us -> 1.29 us
  local copies, waits for them, and re-layouts: 2.56 us -> 0 us
    pallas_call x1 -> x2, Pallas kernels: 182 us -> 159 us  [the longest x1 152 us: per_device_fused(): pl.pallas_call(fused_kernel, out_shape=(pltpu.VMEM((128, 2048), F32), plt...]
    convert_element_type x2 -> x0, other arithmetic: 12.3 us -> none  [the longest x1 11.8 us: per_device_fused(): return (outputs, d_features, d_weight.astype(F32), d_bias.reshape(2048))]
    unnamed x11 -> x0, local copies, waits for them, and re-layouts: 2.56 us -> none
where the time goes in v2:
time: 164 us; the launch traced here: 162 us
  Pallas kernels  159 us (97%)
    pallas_call x1, Pallas kernels, per_device_fused(): pl.pallas_call(fused_kernel, out_shape=(pltpu.VMEM((128, 2048), F32), plt...  152 us
    pallas_call x1, Pallas kernels, per_device_fused(): pl.pallas_call(widen_kernel, grid=(8,), out_shape=(jax.ShapeDtypeStruct((...  7.13 us

profile of v2, /device:TPU:8, one launch (start us, length us, event | category | flops | bytes accessed | tf_op | source)
XLA Modules:
  0.0 161.9 jit_solution(13347753989088664777)
XLA Ops:
  1.3 1.3 reshape.23
  2.6 152.2 %shard_map.111 = (f32[128,2048]{1,0:T(8,128)S(1)}, f32[2048,128]{1,0:T(8,128)S(1)}, bf16[64,128,512]{2,1,0:T(8,128)(2,1)S(1)}, f32[16,128]{1,0:T(8,128)S(1)}) custom-call(s32[32]{0:T(128)} %bitcast.11, s32[1]{0:T(128)} %bitcast.6.count_ref, bf16[32,128,128]{2,1,0:T(8,128)(2,1)} %bitcast.8, bf16[2048,128]{1,0:T(8,128)(2,1)} %feat_ref.1, ...), custom_call_target="tpu_custom_call" | custom-call | flops 7600000000 | bytes 25165824 | tf_op jit(solution)/shard_map/pallas_call | solution.py:584
  154.8 7.1 %shard_map.112 = (f32[2048,2048]{1,0:T(8,128)}, f32[128,2048]{1,0:T(8,128)}, f32[2048,128]{1,0:T(8,128)}, f32[16,128]{1,0:T(8,128)}) custom-call(bf16[64,128,512]{2,1,0:T(8,128)(2,1)S(1)} %get-tuple-element.12.dw_ref, f32[128,2048]{1,0:T(8,128)S(1)} %get-tuple-element.13.out_ref, f32[2048,128]{1,0:T(8,128)S(1)} %get-tuple-element.14.dfeat_ref, ...), custom_call_target="tpu_custom_call" | custom-call | tf_op jit(solution)/shard_map/pallas_call | solution.py:632

commit v3 on v2

--- a/solution.py
+++ b/solution.py
@@ -9,6 +9,7 @@
 F32 = jnp.float32
 BF16 = jnp.bfloat16
 MIB = 2**20
+NC = 2
 
 
 def dense_block(tiles, ids, count, tile_rows, tile_cols):
@@ -60,7 +61,7 @@
     ids_ref, count_ref, tiles_ref, feat_ref, w_ref, bias_ref, scale_ref, cot_ref,
     out_ref, dfeat_ref, dw_ref, db_ref,
     adj, hid, wv, sbuf, scol, xs, xr, keep, lay, xrow, pre, pt, ptg, dls, dlq,
-    dwf, dwp, dwr, dff, dfp, agg, fin, bsum, ssem, rsem, lsem,
+    dwf, dwp, dwr, dff, dfp, agg, fin, bsum, bias32, ssem, rsem, lsem,
 ):
     r = lax.axis_index("row")
     x = lax.axis_index("col")
@@ -111,7 +112,7 @@
         pending[i] = (dst, rcond)
 
     def recv(i, dst, cond=None):
-        pending.pop(i)
+        pending.pop(i, None)
         c = copy(i, dst, dst, sib)
         when(cond, c.wait_recv)
 
@@ -122,12 +123,11 @@
         return pl.multiple_of(v, n)
 
     barrier = pltpu.get_barrier_semaphore()
-    peers = [at(xx, yy, z, kk) for xx, yy, kk in (
-        (x, y, 1 - k), (x, 1 - y, k), (x, 1 - y, 1 - k), (1 - x, y, k),
-        (1 - x, y, 1 - k), (1 - x, 1 - y, k), (1 - x, 1 - y, 1 - k))]
-    peers += [at(x, y, (z + d) % 4, k) for d in (1, 2, 3)]
-    for peer in peers:
-        pl.semaphore_signal(barrier, inc=1, device_id=peer, device_id_type=MESH)
+    near = [(sib, None), (xn, None), (yn, None), (zr, z <= 2), (zl, z >= 1)]
+    for peer, cond in near:
+        when(cond, lambda peer=peer: pl.semaphore_signal(
+            barrier, inc=1, device_id=peer, device_id_type=MESH
+        ))
 
     w_copy = pltpu.make_async_copy(w_ref, wv, lsem.at[0])
     h_copy = pltpu.make_async_copy(feat_ref, hid.at[z], lsem.at[1])
@@ -146,15 +146,16 @@
             )
     for i in range(4):
         sbuf[q, 2 * i:2 * i + 2, :] = scale_ref[...]
+    bias32[...] = bias_ref[...].astype(F32)
     h_copy.wait()
     w_copy.start()
-    pl.semaphore_wait(barrier, len(peers))
+    pl.semaphore_wait(barrier, jnp.where(ends, 4, 5))
 
     def h_part(s, c):
-        return hid.at[s, pl.ds(c * 1024, 1024)]
-
-    right = {(d, c): new() for d in (1, 2, 3) for c in (0, 1)}
-    left = {(d, c): new() for d in (1, 2, 3) for c in (0, 1)}
+        return hid.at[s, pl.ds(c * (2048 // NC), 2048 // NC)]
+
+    right = {(d, c): new() for d in (1, 2, 3) for c in range(NC)}
+    left = {(d, c): new() for d in (1, 2, 3) for c in range(NC)}
 
     def line_send(ids, part, d, c, own_ok=True):
         sr, sl = jnp.maximum(z - (d - 1), 0), jnp.minimum(z + d - 1, 3)
@@ -167,12 +168,12 @@
         recv(ids[1][d, c], part(sl, c), z <= 3 - d)
 
     hz = (right, left)
-    line_send(hz, h_part, 1, 0)
-    line_send(hz, h_part, 1, 1)
+    for c in range(NC):
+        line_send(hz, h_part, 1, c)
 
     s_id = [new() for _ in range(3)]
-    for i, to in zip(s_id, (yn, sib, dg)):
-        send(i, sbuf.at[q], sbuf.at[q], to)
+    send(s_id[0], sbuf.at[q], sbuf.at[q], yn)
+    send(s_id[1], sbuf.at[q], sbuf.at[q], sib)
 
     def a_part(qq, c):
         return adj.at[pl.ds(mult(c * 512 + qq * 128, 128), 128)]
@@ -185,24 +186,24 @@
     for c in range(2):
         send(asib[c], a_part(q, c), a_part(q, c), sib)
 
-    line_recv(hz, h_part, 1, 0)
-    line_send(hz, h_part, 2, 0)
-    line_recv(hz, h_part, 1, 1)
-    line_send(hz, h_part, 2, 1)
+    for c in range(NC):
+        line_recv(hz, h_part, 1, c)
+        line_send(hz, h_part, 2, c)
     recv(ay[0], a_part(q_y, 0))
     send(afwd[0], a_part(q_y, 0), a_part(q_y, 0), sib)
 
-    for i, qq in zip(s_id, (q_y, q_s, q_d)):
-        recv(i, sbuf.at[qq])
+    recv(s_id[0], sbuf.at[q_y])
+    send(s_id[2], sbuf.at[q_y], sbuf.at[q_y], sib)
+    recv(s_id[1], sbuf.at[q_s])
+    recv(s_id[2], sbuf.at[q_d])
     inside = jnp.where(x == z // 2, 1.0, 0.0)
     for b in range(8):
         row = sbuf[b % 4, b // 4:b // 4 + 1, :] * inside
         scol[b] = jnp.broadcast_to(row, (128, 128)).T
 
-    line_recv(hz, h_part, 2, 0)
-    line_send(hz, h_part, 3, 0)
-    line_recv(hz, h_part, 2, 1)
-    line_send(hz, h_part, 3, 1)
+    for c in range(NC):
+        line_recv(hz, h_part, 2, c)
+        line_send(hz, h_part, 3, c)
     recv(ay[1], a_part(q_y, 1))
     send(afwd[1], a_part(q_y, 1), a_part(q_y, 1), sib)
     for c in range(2):
@@ -210,37 +211,51 @@
     for c in range(2):
         recv(afwd[c], a_part(q_d, c))
 
-    x_id = [new() for _ in range(4)]
+    n_parts = (1, 1, 1, 2)
+    x_id = [[new() for _ in range(n)] for n in n_parts]
     l_id = [new() for _ in range(4)]
     row_id = [[new() for _ in range(3)] for _ in range(4)]
     w_waited = []
 
+    def row_part(o, u):
+        return (0, 512) if n_parts[o] == 1 else ((1 - y if u == 0 else y) * 256, 256)
+
     def aggregate(o):
         s = slice_at(o)
         for c, sending in ((1 - x, True), (x, False)):
-            acc = jnp.dot(
-                adj[pl.ds(mult(c * 512, 512), 512), :], hid[s], preferred_element_type=F32
-            )
-            own = []
-            for qq in range(4):
-                first = mult((z % 2) * 1024 + qq * 256 + c * 128, 128)
-                own.append(scol[c * 4 + qq] * hid[s, pl.ds(first, 128), :].astype(F32))
-            acc = acc + jnp.concatenate(own, axis=0)
-            if sending:
-                xs[o] = acc.astype(BF16)
-                send(x_id[o], xs.at[o], xr.at[o], xn)
-            else:
-                keep[o] = acc
+            for u in range(n_parts[o]):
+                first, n = row_part(o, u)
+                rows = pl.ds(mult(first, 256), n)
+                acc = jnp.dot(
+                    adj[pl.ds(mult(c * 512 + first, 256), n), :], hid[s],
+                    preferred_element_type=F32,
+                )
+                own = []
+                for i in range(n // 128):
+                    qq = first // 128 + i
+                    at_node = mult((z % 2) * 1024 + qq * 256 + c * 128, 128)
+                    own.append(scol[c * 4 + qq] * hid[s, pl.ds(at_node, 128), :].astype(F32))
+                acc = acc + jnp.concatenate(own, axis=0)
+                if sending:
+                    xs[o, rows] = acc.astype(BF16)
+                    send(x_id[o][u], xs.at[o, rows], xr.at[o, rows], xn)
+                else:
+                    keep[o, rows] = acc
 
     def combine(o):
         s = slice_at(o)
-        recv(x_id[o], xr.at[o])
-        mine = pl.ds(mult(x * 512, 512), 512)
-        lay[s, mine, :] = (keep[o] + xr[o].astype(F32)).astype(BF16)
-        for i, qq, to in zip(row_id[o], (q_y, q_d, q_s), (yn, dg, sib)):
-            rows = pl.ds(mult(x * 512 + qq * 128, 128), 128)
-            send(i, lay.at[s, rows], xrow.at[s * 4 + q], to)
-        send(l_id[o], lay.at[s, mine], lay.at[s, mine], xn)
+        sends = list(zip(row_id[o], (q_y, q_d, q_s), (yn, dg, sib)))
+        for u in range(n_parts[o]):
+            first, n = row_part(o, u)
+            rows = pl.ds(mult(first, 256), n)
+            recv(x_id[o][u], xr.at[o, rows])
+            mine = pl.ds(mult(x * 512 + first, 256), n)
+            lay[s, mine, :] = (keep[o, rows] + xr[o, rows].astype(F32)).astype(BF16)
+            for i, qq, to in (sends if n_parts[o] == 1 else (sends[:2], sends[2:])[u]):
+                piece_rows = pl.ds(mult(x * 512 + qq * 128, 128), 128)
+                send(i, lay.at[s, piece_rows], xrow.at[s * 4 + q], to)
+        half = pl.ds(mult(x * 512, 512), 512)
+        send(l_id[o], lay.at[s, half], lay.at[s, half], xn)
         xrow[s * 4 + q] = lay[s, pl.ds(mult(x * 512 + q * 128, 128), 128), :]
 
     def linear(o):
@@ -250,43 +265,43 @@
         if not w_waited:
             w_copy.wait()
             w_waited.append(True)
-        part = jnp.concatenate([xrow[s * 4 + i] for i in range(4)], axis=1)
-
-        @pl.loop(0, 4)
+        block = jnp.concatenate([xrow[s * 4 + i] for i in range(4)], axis=1)
+
+        @pl.loop(0, 2)
         def _(t):
-            cols = pl.ds(mult(t * 512, 512), 512)
+            cols = pl.ds(mult(t * 1024, 1024), 1024)
             prod = jnp.dot(
-                part, wv[pl.ds(mult(s * 512, 512), 512), cols], preferred_element_type=F32
+                block, wv[pl.ds(mult(s * 512, 512), 512), cols], preferred_element_type=F32
             )
             if o == 0:
-                pre[:, cols] = prod + bias_ref[:, cols]
+                pre[:, cols] = prod
             else:
                 pre[:, cols] += prod
 
     aggregate(0)
     aggregate(1)
+    aggregate(2)
     combine(0)
-    aggregate(2)
     combine(1)
     linear(0)
+    for c in range(NC):
+        line_recv(hz, h_part, 3, c)
+    aggregate(3)
     combine(2)
     linear(1)
-    line_recv(hz, h_part, 3, 0)
-    line_recv(hz, h_part, 3, 1)
-    aggregate(3)
     linear(2)
     combine(3)
     linear(3)
 
-    def p_half(c):
-        return pt.at[pl.ds(mult(c * 1024, 1024), 1024)]
-
-    def activate(c):
-        @pl.loop(0, 8)
+    def p_part(c, h):
+        return pt.at[pl.ds(mult(c * 1024 + h * 512, 512), 512)]
+
+    def activate(c, h):
+        @pl.loop(0, 4)
         def _(i):
-            t = c * 8 + i
+            t = c * 8 + h * 4 + i
             cols = pl.ds(mult(t * 128, 128), 128)
-            v = pre[:, cols]
+            v = pre[:, cols] + bias32[pl.ds(t, 1), :]
             sig = jax.nn.sigmoid(v)
             out_ref[:, cols] = v * sig
             slope = sig * (1.0 + v * (1.0 - sig))
@@ -295,15 +310,40 @@
             bsum[0, pl.ds(t, 1), :] = jnp.sum(d32, axis=0, keepdims=True)
 
     b_own, b_x = x * 4 + q, (1 - x) * 4 + q
-    px, py, pyf, ps, psf, pd, pdf = (new() for _ in range(7))
+    px, py, pyf, ps, psf, pd, pdf = ([new(), new()] for _ in range(7))
     b_ids = [new() for _ in range(6)]
-    activate(1 - x)
-    send(px, p_half(1 - x), ptg.at[b_own], xn)
-    activate(x)
-    send(py, p_half(x), ptg.at[b_own], yn)
-    send(ps, p_half(x), ptg.at[b_own], sib)
-    send(b_ids[0], bsum.at[0], bsum.at[1], xn)
-    ptg[b_own] = pt[pl.ds(mult(x * 1024, 1024), 1024), :]
+
+    def p_at(b, h):
+        return ptg.at[b, pl.ds(h * 512, 512)]
+
+    def p_send(h):
+        send(px[h], p_part(1 - x, h), p_at(b_own, h), xn)
+        send(py[h], p_part(x, h), p_at(b_own, h), yn)
+        send(ps[h], p_part(x, h), p_at(b_own, h), sib)
+        ptg[b_own, h * 512:(h + 1) * 512] = pt[pl.ds(mult(x * 1024 + h * 512, 512), 512), :]
+
+    def p_relay_x(h):
+        recv(px[h], p_at(b_x, h))
+        send(pyf[h], p_at(b_x, h), p_at(b_x, h), yn)
+        send(psf[h], p_at(b_x, h), p_at(b_x, h), sib)
+        recv(py[h], p_at(x * 4 + q_y, h))
+        send(pd[h], p_at(x * 4 + q_y, h), p_at(x * 4 + q_y, h), sib)
+
+    def p_relay_y(h):
+        recv(pyf[h], p_at((1 - x) * 4 + q_y, h))
+        send(pdf[h], p_at((1 - x) * 4 + q_y, h), p_at((1 - x) * 4 + q_y, h), sib)
+
+    def p_last(h):
+        recv(ps[h], p_at(x * 4 + q_s, h))
+        recv(psf[h], p_at((1 - x) * 4 + q_s, h))
+        recv(pd[h], p_at(x * 4 + q_d, h))
+        recv(pdf[h], p_at((1 - x) * 4 + q_d, h))
+
+    activate(1 - x, 0)
+    activate(x, 0)
+    p_send(0)
+    activate(1 - x, 1)
+    activate(x, 1)
 
     @pl.loop(0, 2)
     def _(i):
@@ -326,31 +366,23 @@
             xx, yy, kk = dl_to[i]
             send(dl_ids[i], dls.at[2 * yy + kk], dlq.at[b_own], at(xx, yy, z, kk))
 
-    recv(px, ptg.at[b_x])
-    send(pyf, ptg.at[b_x], ptg.at[b_x], yn)
+    p_send(1)
+    send(b_ids[0], bsum.at[0], bsum.at[1], xn)
+    dlq[b_own] = dls[q]
+    p_relay_x(0)
     send_layer_grad((0, 1, 2))
-    send(psf, ptg.at[b_x], ptg.at[b_x], sib)
+    p_relay_x(1)
+    p_relay_y(0)
     recv(b_ids[0], bsum.at[1])
     bsum[2] = bsum[0] + bsum[1]
     send(b_ids[1], bsum.at[2], bsum.at[3], yn)
-    dlq[b_own] = dls[q]
-    recv(py, ptg.at[x * 4 + q_y])
-    send(pd, ptg.at[x * 4 + q_y], ptg.at[x * 4 + q_y], sib)
-    recv(pyf, ptg.at[(1 - x) * 4 + q_y])
-    send(pdf, ptg.at[(1 - x) * 4 + q_y], ptg.at[(1 - x) * 4 + q_y], sib)
-    send_layer_grad((3, 4, 5, 6))
-    recv(b_ids[1], bsum.at[3])
-    bsum[4] = bsum[2] + bsum[3]
-    send(b_ids[2], bsum.at[4], bsum.at[5], sib)
-    recv(ps, ptg.at[x * 4 + q_s])
-    recv(psf, ptg.at[(1 - x) * 4 + q_s])
-    recv(pd, ptg.at[x * 4 + q_d])
-    recv(pdf, ptg.at[(1 - x) * 4 + q_d])
     for o in range(4):
         recv(l_id[o], lay.at[slice_at(o), pl.ds(mult((1 - x) * 512, 512), 512)])
+    p_last(0)
 
     dw_ids = [[new() for _ in range(3)] for _ in range(2)]
-    for h in range(2):
+
+    def weight_grad(h):
         rows = pl.ds(h * 512, 512)
         lhs = jnp.concatenate([ptg[b, rows, :] for b in range(8)], axis=1)
         rhs = jnp.concatenate([lay[s] for s in range(4)], axis=1)
@@ -361,13 +393,23 @@
         for d in (2, 1, 3):
             to = (z + d) % 4
             send(dw_ids[h][d - 1], dwp.at[to, rows], dwr.at[z, rows], at(x, y, to, k))
+
+    weight_grad(0)
+    p_relay_y(1)
+    send_layer_grad((3, 4, 5, 6))
+    recv(b_ids[1], bsum.at[3])
+    bsum[4] = bsum[2] + bsum[3]
+    send(b_ids[2], bsum.at[4], bsum.at[5], sib)
+    p_last(1)
+    weight_grad(1)
     recv(b_ids[2], bsum.at[5])
     bsum[6] = bsum[4] + bsum[5]
     for d in (1, 2, 3):
         send(b_ids[2 + d], bsum.at[6], bsum.at[6 + d], at(x, y, (z + d) % 4, k))
 
-    for i, (xx, yy, kk) in zip(dl_ids, dl_to):
-        recv(i, dlq.at[xx * 4 + 2 * yy + kk])
+    def layer_grads_here(cond):
+        for i, (xx, yy, kk) in zip(dl_ids, dl_to):
+            recv(i, dlq.at[xx * 4 + 2 * yy + kk], cond)
 
     pair = z // 2
     e, m = 3 * pair, 1 + pair
@@ -398,9 +440,12 @@
                 dfp[first + i, :, cols] = acc[i * 128:(i + 1) * 128].astype(BF16)
 
     mid_dev, end_dev = at(x, y, m, k), at(x, y, e, k)
-    input_grad(2 * pair)
+    layer_grads_here(mids)
+
+    @pl.when(mids)
+    def _():
+        input_grad(2 * pair)
     send(f_fin[0], dfp.at[e], fin.at[0], end_dev, mids, ends)
-    input_grad(2 * (1 - pair))
 
     def cut(c):
         return pl.ds(c * 1024, 1024)
@@ -428,9 +473,8 @@
         return dw_ref.at[(s * 4 + qq) * 4 + c * 2 + h]
 
     gz = tuple({(d, h): new() for d in (1, 2, 3) for h in (0, 1)} for _ in range(2))
-    gx, gy, gs, gxy, gyx, gsx, gsy, gsd1, gsd2 = (
-        {(h, o): new() for h in (0, 1) for o in range(4)} for _ in range(9)
-    )
+    gx, gy, gxy, gyx = ({(h, o): new() for h in (0, 1) for o in range(4)} for _ in range(4))
+    gs, gsd = ([new() for _ in range(4)] for _ in range(2))
 
     def z_piece(s, h):
         return piece(s, q, x, h)
@@ -451,7 +495,9 @@
         src = piece(slice_at(o), q, x, h)
         send(gx[h, o], src, src, xn)
         send(gy[h, o], src, src, yn)
-        send(gs[h, o], src, src, sib)
+
+    def whole(s, qq):
+        return dw_ref.at[pl.ds((s * 4 + qq) * 4, 4)]
 
     def part(ref, i):
         return ref.at[pl.ds(i * 64, 64)]
@@ -461,26 +507,21 @@
         from_x, from_y = piece(s, q, 1 - x, h), piece(s, q_y, x, h)
         recv(gx[h, o], from_x)
         send(gxy[h, o], part(from_x, 0), part(from_x, 0), yn)
-        send(gsx[h, o], from_x, from_x, sib)
+        if h == 1:
+            send(gs[o], whole(s, q), whole(s, q), sib)
         recv(gy[h, o], from_y)
         send(gyx[h, o], part(from_y, 1), part(from_y, 1), xn)
-        send(gsy[h, o], from_y, from_y, sib)
 
     def relay_diag(h, o):
         block = piece(slice_at(o), q_y, 1 - x, h)
         recv(gxy[h, o], part(block, 0))
-        send(gsd1[h, o], part(block, 0), part(block, 0), sib)
         recv(gyx[h, o], part(block, 1))
-        send(gsd2[h, o], part(block, 1), part(block, 1), sib)
-
-    def last(h, o):
-        s = slice_at(o)
-        recv(gs[h, o], piece(s, q_s, x, h))
-        recv(gsx[h, o], piece(s, q_s, 1 - x, h))
-        recv(gsy[h, o], piece(s, q_d, x, h))
-        block = piece(s, q_d, 1 - x, h)
-        recv(gsd1[h, o], part(block, 0))
-        recv(gsd2[h, o], part(block, 1))
+        if h == 1:
+            send(gsd[o], whole(slice_at(o), q_y), whole(slice_at(o), q_y), sib)
+
+    def last(o):
+        recv(gs[o], whole(slice_at(o), q_s))
+        recv(gsd[o], whole(slice_at(o), q_d))
 
     def along(h, d):
         line_recv(gz, z_piece, d, h)
@@ -489,6 +530,12 @@
         spread(h, d)
 
     finish(0)
+    layer_grads_here(ends)
+    input_grad(2 * (1 - pair))
+
+    @pl.when(ends)
+    def _():
+        input_grad(2 * pair)
     along(0, 1)
     relay(0, 0)
     finish(1)
@@ -540,41 +587,35 @@
         tot = dff[z, :, cols] + fin[0, :, cols].astype(F32) + fin[1, :, cols].astype(F32)
         dfeat_ref[pl.ds(mult(t * 128, 128), 128), :] = tot.T
 
-    for h in range(2):
-        for o in range(4):
-            last(h, o)
-    assert not pending
+    for o in range(4):
+        last(o)
+    assert not pending and count[0] <= N_SEMS, count
     for i, (c, cond) in sent_by.items():
         when(cond, c.wait_send)
 
 
-def widen_kernel(dw_ref, out_ref, dfeat_ref, db_ref, dw_out, out_out, dfeat_out, db_out, sem):
-    step = pl.program_id(0)
+def widen_kernel(dw_ref, out_ref, dfeat_ref, db_ref, dw_out, out_out, dfeat_out, db_out, wide, sem):
     copies = [
-        pltpu.make_async_copy(src, dst, sem.at[i])
+        pltpu.make_async_copy(src, dst, sem.at[16 + i])
         for i, (src, dst) in enumerate(
             ((out_ref, out_out), (dfeat_ref, dfeat_out), (db_ref, db_out))
         )
     ]
-
-    @pl.when(step == 0)
-    def _():
-        for c in copies:
-            c.start()
-
-    for i in range(2):
+    for c in copies:
+        c.start()
+    rows = [
+        pltpu.make_async_copy(wide.at[i], dw_out.at[pl.ds(i * 128, 128)], sem.at[i])
+        for i in range(16)
+    ]
+    for i in range(16):
         for j in range(4):
-            dw_out[i * 128:(i + 1) * 128, j * 512:(j + 1) * 512] = (
-                dw_ref[(2 * step + i) * 4 + j].astype(F32)
-            )
-
-    @pl.when(step == pl.num_programs(0) - 1)
-    def _():
-        for c in copies:
-            c.wait()
-
-
-N_SEMS = 180
+            wide[i, :, j * 512:(j + 1) * 512] = dw_ref[4 * i + j].astype(F32)
+        rows[i].start()
+    for c in copies + rows:
+        c.wait()
+
+
+N_SEMS = 137
 
 
 def per_device_fused(features, weight, bias, self_scale, adj_tiles, tile_ids, tile_counts, cotangent):
@@ -615,6 +656,7 @@
             pltpu.VMEM((2, 128, 2048), BF16),
             pltpu.VMEM((2, 128, 2048), BF16),
             pltpu.VMEM((10, 16, 128), F32),
+            pltpu.VMEM((16, 128), F32),
             pltpu.SemaphoreType.DMA((N_SEMS,)),
             pltpu.SemaphoreType.DMA((N_SEMS,)),
             pltpu.SemaphoreType.DMA((3,)),
@@ -627,11 +669,10 @@
         ),
     )(
         tile_ids[0, 0], tile_counts[0], adj_tiles[0, 0], features, weight,
-        bias.astype(F32).reshape(1, 2048), self_scale.reshape(2, 128), cotangent,
+        bias.reshape(16, 128), self_scale.reshape(2, 128), cotangent,
     )
     d_weight, outputs, d_features, d_bias = pl.pallas_call(
         widen_kernel,
-        grid=(8,),
         out_shape=(
             jax.ShapeDtypeStruct((2048, 2048), F32),
             jax.ShapeDtypeStruct((128, 2048), F32),
@@ -639,9 +680,9 @@
             jax.ShapeDtypeStruct((16, 128), F32),
         ),
         in_specs=[vmem] * 4,
-        out_specs=(pl.BlockSpec((256, 2048), lambda i: (i, 0)), hbm, hbm, hbm),
-        scratch_shapes=[pltpu.SemaphoreType.DMA((3,))],
-        compiler_params=pltpu.CompilerParams(vmem_limit_bytes=20 * MIB),
+        out_specs=(hbm, hbm, hbm, hbm),
+        scratch_shapes=[pltpu.VMEM((16, 128, 2048), F32), pltpu.SemaphoreType.DMA((19,))],
+        compiler_params=pltpu.CompilerParams(vmem_limit_bytes=30 * MIB),
     )(gathered, outputs, d_features, d_bias)
     return outputs, d_features, d_weight, d_bias.reshape(2048)
 

time: 164 us -> 153 us (0.933)
  Pallas kernels: 159 us -> 151 us
    pallas_call x1, Pallas kernels: 152 us -> 144 us  [per_device_fused(): pl.pallas_call(fused_kernel, out_shape=(pltpu.VMEM((128, 2048), F32), plt...]
where the time goes in v3:
time: 153 us; the launch traced here: 152 us
  Pallas kernels  151 us (99%)
    pallas_call x1, Pallas kernels, per_device_fused(): pl.pallas_call(fused_kernel, out_shape=(pltpu.VMEM((128, 2048), F32), plt...  144 us
    pallas_call x1, Pallas kernels, per_device_fused(): pl.pallas_call(widen_kernel, out_shape=(jax.ShapeDtypeStruct((2048, 2048)...  6.62 us

profile of v3, /device:TPU:8, one launch (start us, length us, event | category | flops | bytes accessed | tf_op | source)
XLA Modules:
  0.0 152.0 jit_solution(2768835146132975384)
XLA Ops:
  1.3 144.0 %shard_map.111 = (f32[128,2048]{1,0:T(8,128)S(1)}, f32[2048,128]{1,0:T(8,128)S(1)}, bf16[64,128,512]{2,1,0:T(8,128)(2,1)S(1)}, f32[16,128]{1,0:T(8,128)S(1)}) custom-call(s32[32]{0:T(128)} %bitcast.11, s32[1]{0:T(128)} %bitcast.6.count_ref, bf16[32,128,128]{2,1,0:T(8,128)(2,1)} %bitcast.7, bf16[2048,128]{1,0:T(8,128)(2,1)} %feat_ref.1, ...), custom_call_target="tpu_custom_call" | custom-call | flops 7600000000 | bytes 25165824 | tf_op jit(solution)/shard_map/pallas_call | solution.py:625
  145.3 6.6 %shard_map.112 = (f32[2048,2048]{1,0:T(8,128)}, f32[128,2048]{1,0:T(8,128)}, f32[2048,128]{1,0:T(8,128)}, f32[16,128]{1,0:T(8,128)}) custom-call(bf16[64,128,512]{2,1,0:T(8,128)(2,1)S(1)} %get-tuple-element.12.dw_ref, f32[128,2048]{1,0:T(8,128)S(1)} %get-tuple-element.13.out_ref, f32[2048,128]{1,0:T(8,128)S(1)} %get-tuple-element.14.dfeat_ref, ...), custom_call_target="tpu_custom_call" | custom-call | tf_op jit(solution)/shard_map/pallas_call | solution.py:674

commit v4 on v3

--- a/solution.py
+++ b/solution.py
@@ -60,8 +60,8 @@
 def fused_kernel(
     ids_ref, count_ref, tiles_ref, feat_ref, w_ref, bias_ref, scale_ref, cot_ref,
     out_ref, dfeat_ref, dw_ref, db_ref,
-    adj, hid, wv, sbuf, scol, xs, xr, keep, lay, xrow, pre, pt, ptg, dls, dlq,
-    dwf, dwp, dwr, dff, dfp, agg, fin, bsum, bias32, ssem, rsem, lsem,
+    adj, adj_e, hid, wv, sbuf, sbuf_e, scol, xs, xr, keep, lay, xrow, pre, pt, ptg, dls, dlq,
+    dwf, dwp, dwr, dff, dfp, dle, fin, bsum, bias32, ssem, rsem, lsem,
 ):
     r = lax.axis_index("row")
     x = lax.axis_index("col")
@@ -178,19 +178,15 @@
     def a_part(qq, c):
         return adj.at[pl.ds(mult(c * 512 + qq * 128, 128), 128)]
 
-    ay = [new() for _ in range(2)]
-    asib = [new() for _ in range(2)]
-    afwd = [new() for _ in range(2)]
-    for c in range(2):
-        send(ay[c], a_part(q, c), a_part(q, c), yn)
-    for c in range(2):
-        send(asib[c], a_part(q, c), a_part(q, c), sib)
-
-    for c in range(NC):
-        line_recv(hz, h_part, 1, c)
-        line_send(hz, h_part, 2, c)
-    recv(ay[0], a_part(q_y, 0))
-    send(afwd[0], a_part(q_y, 0), a_part(q_y, 0), sib)
+    halves = (1 - x, x)
+    ay, asib, afwd = ([new(), new()] for _ in range(3))
+    for i, c in enumerate(halves):
+        send(asib[i], a_part(q, c), a_part(q, c), sib)
+    send(ay[0], a_part(q, 1 - x), a_part(q, 1 - x), yn)
+
+    line_recv(hz, h_part, 1, 0)
+    line_send(hz, h_part, 2, 0)
+    send(ay[1], a_part(q, x), a_part(q, x), yn)
 
     recv(s_id[0], sbuf.at[q_y])
     send(s_id[2], sbuf.at[q_y], sbuf.at[q_y], sib)
@@ -201,62 +197,65 @@
         row = sbuf[b % 4, b // 4:b // 4 + 1, :] * inside
         scol[b] = jnp.broadcast_to(row, (128, 128)).T
 
-    for c in range(NC):
-        line_recv(hz, h_part, 2, c)
-        line_send(hz, h_part, 3, c)
-    recv(ay[1], a_part(q_y, 1))
-    send(afwd[1], a_part(q_y, 1), a_part(q_y, 1), sib)
+    line_recv(hz, h_part, 1, 1)
+    line_send(hz, h_part, 2, 1)
+
+    pair = z // 2
+    e, m = 3 * pair, 1 + pair
+    e2, m2 = 3 - 3 * pair, 2 - pair
+    mid_dev, end_dev = at(x, y, m, k), at(x, y, e, k)
+
+    def e_part(qq, c):
+        return adj_e.at[pl.ds(mult(c * 512 + qq * 128, 128), 128)]
+
+    ez, ey, esib, efwd = ([new(), new()] for _ in range(4))
+    es = new()
     for c in range(2):
-        recv(asib[c], a_part(q_s, c))
-    for c in range(2):
-        recv(afwd[c], a_part(q_d, c))
-
-    n_parts = (1, 1, 1, 2)
-    x_id = [[new() for _ in range(n)] for n in n_parts]
+        send(ez[c], a_part(q, c), e_part(q, c), mid_dev, ends, mids)
+    send(es, sbuf, sbuf_e, mid_dev, ends, mids)
+
+    x_id = [[new(), new()] for _ in range(4)]
     l_id = [new() for _ in range(4)]
     row_id = [[new() for _ in range(3)] for _ in range(4)]
     w_waited = []
 
-    def row_part(o, u):
-        return (0, 512) if n_parts[o] == 1 else ((1 - y if u == 0 else y) * 256, 256)
-
-    def aggregate(o):
+    def aggregate(o, c, u):
         s = slice_at(o)
-        for c, sending in ((1 - x, True), (x, False)):
-            for u in range(n_parts[o]):
-                first, n = row_part(o, u)
-                rows = pl.ds(mult(first, 256), n)
-                acc = jnp.dot(
-                    adj[pl.ds(mult(c * 512 + first, 256), n), :], hid[s],
-                    preferred_element_type=F32,
-                )
-                own = []
-                for i in range(n // 128):
-                    qq = first // 128 + i
-                    at_node = mult((z % 2) * 1024 + qq * 256 + c * 128, 128)
-                    own.append(scol[c * 4 + qq] * hid[s, pl.ds(at_node, 128), :].astype(F32))
-                acc = acc + jnp.concatenate(own, axis=0)
-                if sending:
-                    xs[o, rows] = acc.astype(BF16)
-                    send(x_id[o][u], xs.at[o, rows], xr.at[o, rows], xn)
-                else:
-                    keep[o, rows] = acc
+        first = (1 - y if u == 0 else y) * 256
+        rows = pl.ds(mult(first, 256), 256)
+        acc = jnp.dot(
+            adj[pl.ds(mult(halves[c] * 512 + first, 256), 256), :], hid[s],
+            preferred_element_type=F32,
+        )
+        own = []
+        for i in range(2):
+            qq = first // 128 + i
+            at_node = mult((z % 2) * 1024 + qq * 256 + halves[c] * 128, 128)
+            own.append(scol[halves[c] * 4 + qq] * hid[s, pl.ds(at_node, 128), :].astype(F32))
+        acc = acc + jnp.concatenate(own, axis=0)
+        if c == 0:
+            xs[o, rows] = acc.astype(BF16)
+            send(x_id[o][u], xs.at[o, rows], xr.at[o, rows], xn)
+        else:
+            keep[o, rows] = acc
 
     def combine(o):
         s = slice_at(o)
         sends = list(zip(row_id[o], (q_y, q_d, q_s), (yn, dg, sib)))
-        for u in range(n_parts[o]):
-            first, n = row_part(o, u)
-            rows = pl.ds(mult(first, 256), n)
+        for u in range(2):
+            first = (1 - y if u == 0 else y) * 256
+            rows = pl.ds(mult(first, 256), 256)
             recv(x_id[o][u], xr.at[o, rows])
-            mine = pl.ds(mult(x * 512 + first, 256), n)
+            mine = pl.ds(mult(x * 512 + first, 256), 256)
             lay[s, mine, :] = (keep[o, rows] + xr[o, rows].astype(F32)).astype(BF16)
-            for i, qq, to in (sends if n_parts[o] == 1 else (sends[:2], sends[2:])[u]):
+            for i, qq, to in (sends[:2], sends[2:])[u]:
                 piece_rows = pl.ds(mult(x * 512 + qq * 128, 128), 128)
                 send(i, lay.at[s, piece_rows], xrow.at[s * 4 + q], to)
-        half = pl.ds(mult(x * 512, 512), 512)
-        send(l_id[o], lay.at[s, half], lay.at[s, half], xn)
         xrow[s * 4 + q] = lay[s, pl.ds(mult(x * 512 + q * 128, 128), 128), :]
+
+    def share(o):
+        half = lay.at[slice_at(o), pl.ds(mult(x * 512, 512), 512)]
+        send(l_id[o], half, half, xn)
 
     def linear(o):
         s = slice_at(o)
@@ -278,19 +277,40 @@
             else:
                 pre[:, cols] += prod
 
-    aggregate(0)
-    aggregate(1)
-    aggregate(2)
-    combine(0)
-    combine(1)
+    for i in range(2):
+        recv(asib[i], a_part(q_s, halves[i]))
+    for o in range(2):
+        aggregate(o, 0, 1)
+        aggregate(o, 1, 1)
+    recv(ay[0], a_part(q_y, 1 - x))
+    send(afwd[0], a_part(q_y, 1 - x), a_part(q_y, 1 - x), sib)
+    recv(afwd[0], a_part(q_d, 1 - x))
+    aggregate(0, 0, 0)
+    line_recv(hz, h_part, 2, 0)
+    line_send(hz, h_part, 3, 0)
+    aggregate(1, 0, 0)
+    line_recv(hz, h_part, 2, 1)
+    line_send(hz, h_part, 3, 1)
+    for c, u in ((0, 0), (0, 1), (1, 1)):
+        aggregate(2, c, u)
+    recv(ay[1], a_part(q_y, x))
+    send(afwd[1], a_part(q_y, x), a_part(q_y, x), sib)
+    recv(afwd[1], a_part(q_d, x))
+    for o in range(3):
+        aggregate(o, 1, 0)
+        combine(o)
+        if o < 2:
+            share(o)
     linear(0)
+    linear(1)
     for c in range(NC):
         line_recv(hz, h_part, 3, c)
-    aggregate(3)
-    combine(2)
-    linear(1)
+    for c, u in ((0, 0), (0, 1), (1, 0), (1, 1)):
+        aggregate(3, c, u)
     linear(2)
     combine(3)
+    share(3)
+    share(2)
     linear(3)
 
     def p_part(c, h):
@@ -402,6 +422,10 @@
     send(b_ids[2], bsum.at[4], bsum.at[5], sib)
     p_last(1)
     weight_grad(1)
+    for c in range(2):
+        recv(ez[c], e_part(q, c), mids)
+        send(ey[c], e_part(q, c), e_part(q, c), yn, mids, mids)
+        send(esib[c], e_part(q, c), e_part(q, c), sib, mids, mids)
     recv(b_ids[2], bsum.at[5])
     bsum[6] = bsum[4] + bsum[5]
     for d in (1, 2, 3):
@@ -411,63 +435,83 @@
         for i, (xx, yy, kk) in zip(dl_ids, dl_to):
             recv(i, dlq.at[xx * 4 + 2 * yy + kk], cond)
 
-    pair = z // 2
-    e, m = 3 * pair, 1 + pair
-    e2, m2 = 3 - 3 * pair, 2 - pair
-    f_in = [[new() for _ in range(2)] for _ in range(2)]
-    f_out = [[new() for _ in range(2)] for _ in range(2)]
-    f_fin = [new() for _ in range(2)]
-
-    def input_grad(first):
+    f_in = [new() for _ in range(3)]
+    f_out = [new() for _ in range(2)]
+    f_fin = new()
+    own_half = x == z // 2
+
+    def grads(dl, a, scale, at_z, first, n, t, width):
+        cols = pl.ds(mult(t * width, width), width)
         lhs = jnp.concatenate(
-            [dlq[b, pl.ds(first, 2)].reshape(256, 128) for b in range(8)], axis=1
+            [dl[b, pl.ds(first, n)].reshape(n * 128, 128) for b in range(8)], axis=1
         )
-
+        acc = jnp.dot(lhs, a[:, cols], preferred_element_type=F32)
+        per = width // 256
+        own = jnp.where(own_half & (t // (4 // per) == at_z % 2), 1.0, 0.0)
+        diag = []
+        for j in range(per):
+            qq = (t % (4 // per)) * per + j
+            for c in range(2):
+                row = scale[qq, c:c + 1, :] * own
+                diag.append(
+                    dl[c * 4 + qq, pl.ds(first, n)].reshape(n * 128, 128).astype(F32) * row
+                )
+        return acc + jnp.concatenate(diag, axis=1), cols
+
+    def grads_here(first, n):
         @pl.loop(0, 4)
         def _(t):
-            cols = pl.ds(mult(t * 512, 512), 512)
-            acc = jnp.dot(lhs, adj[:, cols], preferred_element_type=F32)
-            own = jnp.where((x == z // 2) & (t // 2 == z % 2), 1.0, 0.0)
-            diag = []
-            for j in range(2):
-                qq = (t % 2) * 2 + j
-                for c in range(2):
-                    row = sbuf[qq, c:c + 1, :] * own
-                    diag.append(dlq[c * 4 + qq, pl.ds(first, 2)].reshape(256, 128).astype(F32) * row)
-            acc = acc + jnp.concatenate(diag, axis=1)
-            for i in range(2):
+            acc, cols = grads(dlq, adj, sbuf, z, first, n, t, 512)
+            for i in range(n):
                 dff[first + i, :, cols] = acc[i * 128:(i + 1) * 128]
-                dfp[first + i, :, cols] = acc[i * 128:(i + 1) * 128].astype(BF16)
-
-    mid_dev, end_dev = at(x, y, m, k), at(x, y, e, k)
+
+    def grads_end(s):
+        @pl.loop(0, 4)
+        def _(t):
+            acc, cols = grads(dle, adj_e, sbuf_e, e, s, 1, t, 512)
+            tot = dff[s, :, cols] + acc
+            dff[s, :, cols] = tot
+            dfp[s, :, cols] = tot.astype(BF16)
+
     layer_grads_here(mids)
 
     @pl.when(mids)
     def _():
-        input_grad(2 * pair)
-    send(f_fin[0], dfp.at[e], fin.at[0], end_dev, mids, ends)
-
-    def cut(c):
-        return pl.ds(c * 1024, 1024)
-
-    def end_send(j, c):
-        s_to = (m2, e2)[j]
-        send(f_in[j][c], dfp.at[s_to, :, cut(c)], agg.at[j, :, cut(c)], mid_dev, ends, mids)
-
-    def end_wait(j, c):
-        out, cond = sent_by.pop(f_in[j][c])
-        pl.when(cond)(out.wait_send)
-
-    def mid_send(j, c):
-        s_to, to = ((m2, at(x, y, m2, k)), (e2, at(x, y, e2, k)))[j]
-        recv(f_in[j][c], agg.at[j, :, cut(c)], mids)
+        grads_here(2 * pair, 2)
+        dfp[e] = dff[e].astype(BF16)
+    send(f_fin, dfp.at[e], fin.at[0], end_dev, mids, ends)
+
+    @pl.when(mids)
+    def _():
+        grads_here(2 * (1 - pair), 2)
+
+    def end_send():
+        layer_grads_here(ends)
+        for j, s in enumerate((m2, e2, m)):
+            send(f_in[j], dlq.at[:, s], dle.at[:, s], mid_dev, ends, mids)
+
+        @pl.when(ends)
+        def _():
+            grads_here(e, 1)
+
+    def mid_ready():
+        recv(es, sbuf_e, mids)
+        for c in range(2):
+            recv(ey[c], e_part(q_y, c), mids)
+            send(efwd[c], e_part(q_y, c), e_part(q_y, c), sib, mids, mids)
+        for c in range(2):
+            recv(esib[c], e_part(q_s, c), mids)
+            recv(efwd[c], e_part(q_d, c), mids)
+
+    def mid_send(j):
+        s_to = (m2, e2, m)[j]
+        recv(f_in[j], dle.at[:, s_to], mids)
 
         @pl.when(mids)
         def _():
-            dfp[s_to, :, cut(c)] = (
-                dff[s_to, :, cut(c)] + agg[j, :, cut(c)].astype(F32)
-            ).astype(BF16)
-        send(f_out[j][c], dfp.at[s_to, :, cut(c)], fin.at[1, :, cut(c)], to, mids, (mids, ends)[j])
+            grads_end(s_to)
+        if j < 2:
+            send(f_out[j], dfp.at[s_to], fin.at[1], at(x, y, s_to, k), mids, (mids, ends)[j])
 
     def piece(s, qq, c, h):
         return dw_ref.at[(s * 4 + qq) * 4 + c * 2 + h]
@@ -530,40 +574,27 @@
         spread(h, d)
 
     finish(0)
-    layer_grads_here(ends)
-    input_grad(2 * (1 - pair))
-
-    @pl.when(ends)
-    def _():
-        input_grad(2 * pair)
+    end_send()
+    mid_ready()
     along(0, 1)
     relay(0, 0)
     finish(1)
-    end_send(0, 0)
-    end_send(0, 1)
     along(0, 2)
     relay(0, 1)
     relay_diag(0, 0)
     along(1, 1)
-    mid_send(0, 0)
-    end_wait(0, 0)
-    end_send(1, 0)
+    mid_send(0)
     relay(1, 0)
     relay_diag(0, 1)
     along(0, 3)
-    mid_send(0, 1)
-    end_wait(0, 1)
-    end_send(1, 1)
+    mid_send(1)
     relay(0, 2)
     relay_diag(1, 0)
     along(1, 2)
-    mid_send(1, 0)
-    end_wait(1, 0)
-    send(f_fin[1], dfp.at[m], fin.at[0], mid_dev, ends, mids)
     relay(1, 1)
     relay_diag(0, 2)
     along(1, 3)
-    mid_send(1, 1)
+    mid_send(2)
     relay(0, 3)
     relay_diag(1, 1)
     relay(1, 2)
@@ -575,16 +606,15 @@
         recv(b_ids[2 + d], bsum.at[6 + d])
     db_ref[...] = bsum[6] + bsum[7] + bsum[8] + bsum[9]
 
-    recv(f_fin[0], fin.at[0], ends)
-    recv(f_fin[1], fin.at[0], mids)
-    for c in range(2):
-        recv(f_out[0][c], fin.at[1, :, cut(c)], mids)
-        recv(f_out[1][c], fin.at[1, :, cut(c)], ends)
+    recv(f_fin, fin.at[0], ends)
+    recv(f_out[0], fin.at[1], mids)
+    recv(f_out[1], fin.at[1], ends)
 
     @pl.loop(0, 16)
     def _(t):
         cols = pl.ds(mult(t * 128, 128), 128)
-        tot = dff[z, :, cols] + fin[0, :, cols].astype(F32) + fin[1, :, cols].astype(F32)
+        first = jnp.where(ends, fin[0, :, cols].astype(F32), 0.0)
+        tot = dff[z, :, cols] + first + fin[1, :, cols].astype(F32)
         dfeat_ref[pl.ds(mult(t * 128, 128), 128), :] = tot.T
 
     for o in range(4):
@@ -615,7 +645,7 @@
         c.wait()
 
 
-N_SEMS = 137
+N_SEMS = 145
 
 
 def per_device_fused(features, weight, bias, self_scale, adj_tiles, tile_ids, tile_counts, cotangent):
@@ -634,8 +664,10 @@
         out_specs=(vmem, vmem, vmem, vmem),
         scratch_shapes=[
             pltpu.VMEM((1024, 2048), BF16),
+            pltpu.VMEM((1024, 2048), BF16),
             pltpu.VMEM((4, 2048, 128), BF16),
             pltpu.VMEM((2048, 2048), BF16),
+            pltpu.VMEM((4, 8, 128), F32),
             pltpu.VMEM((4, 8, 128), F32),
             pltpu.VMEM((8, 128, 128), F32),
             pltpu.VMEM((4, 512, 128), BF16),
@@ -653,7 +685,7 @@
             pltpu.VMEM((4, 1024, 128), BF16),
             pltpu.VMEM((4, 128, 2048), F32),
             pltpu.VMEM((4, 128, 2048), BF16),
-            pltpu.VMEM((2, 128, 2048), BF16),
+            pltpu.VMEM((8, 4, 128, 128), BF16),
             pltpu.VMEM((2, 128, 2048), BF16),
             pltpu.VMEM((10, 16, 128), F32),
             pltpu.VMEM((16, 128), F32),
@@ -662,7 +694,7 @@
             pltpu.SemaphoreType.DMA((3,)),
         ],
         compiler_params=pltpu.CompilerParams(
-            collective_id=0, has_side_effects=True, vmem_limit_bytes=50 * MIB
+            collective_id=0, has_side_effects=True, vmem_limit_bytes=53 * MIB
         ),
         cost_estimate=pl.CostEstimate(
             flops=7_600_000_000, bytes_accessed=24 * MIB, transcendentals=262144

time: 153 us -> 146 us (0.954)
  the two profiles are of different devices: /device:TPU:8 before, /device:TPU:0 now
where the time goes in v4:
time: 146 us
  Pallas kernels  145 us (99%)
    pallas_call x1, Pallas kernels, per_device_fused(): pl.pallas_call(fused_kernel, out_shape=(pltpu.VMEM((128, 2048), F32), plt...  138 us
    pallas_call x1, Pallas kernels, per_device_fused(): pl.pallas_call(widen_kernel, out_shape=(jax.ShapeDtypeStruct((2048, 2048)...  6.62 us

profile of v4, /device:TPU:0, one launch (start us, length us, event | category | flops | bytes accessed | tf_op | source)
XLA Modules:
  0.0 145.9 jit_solution(7724319873928367531)
XLA Ops:
  1.3 138.0 %shard_map.111 = (f32[128,2048]{1,0:T(8,128)S(1)}, f32[2048,128]{1,0:T(8,128)S(1)}, bf16[64,128,512]{2,1,0:T(8,128)(2,1)S(1)}, f32[16,128]{1,0:T(8,128)S(1)}) custom-call(s32[32]{0:T(128)} %bitcast.11, s32[1]{0:T(128)} %bitcast.6.count_ref, bf16[32,128,128]{2,1,0:T(8,128)(2,1)} %bitcast.7, bf16[2048,128]{1,0:T(8,128)(2,1)} %feat_ref.1, ...), custom_call_target="tpu_custom_call" | custom-call | flops 7600000000 | bytes 25165824 | tf_op jit(solution)/shard_map/pallas_call | solution.py:655
  139.3 6.6 %shard_map.112 = (f32[2048,2048]{1,0:T(8,128)}, f32[128,2048]{1,0:T(8,128)}, f32[2048,128]{1,0:T(8,128)}, f32[16,128]{1,0:T(8,128)}) custom-call(bf16[64,128,512]{2,1,0:T(8,128)(2,1)S(1)} %get-tuple-element.12.dw_ref, f32[128,2048]{1,0:T(8,128)S(1)} %get-tuple-element.13.out_ref, f32[2048,128]{1,0:T(8,128)S(1)} %get-tuple-element.14.dfeat_ref, ...), custom_call_target="tpu_custom_call" | custom-call | tf_op jit(solution)/shard_map/pallas_call | solution.py:706

commit v5 on v4

--- a/solution.py
+++ b/solution.py
@@ -9,6 +9,17 @@
 F32 = jnp.float32
 BF16 = jnp.bfloat16
 MIB = 2**20
+ORDER = (
+    "H P f0 E0",
+    "a01 r00 R f1",
+    "E2 E1 a02 r01",
+    "d00 a11 M0 r10",
+    "d01 a03 M1 G0",
+    "r02 d10 a12 r03",
+    "r11 d02 a13 M2",
+    "d11 r12 d03 G1",
+    "r13 d12 d13",
+)
 NC = 2
 
 
@@ -208,7 +219,7 @@
     def e_part(qq, c):
         return adj_e.at[pl.ds(mult(c * 512 + qq * 128, 128), 128)]
 
-    ez, ey, esib, efwd = ([new(), new()] for _ in range(4))
+    ez, ezy, esib, efwd = ([new(), new()] for _ in range(4))
     es = new()
     for c in range(2):
         send(ez[c], a_part(q, c), e_part(q, c), mid_dev, ends, mids)
@@ -295,6 +306,8 @@
         aggregate(2, c, u)
     recv(ay[1], a_part(q_y, x))
     send(afwd[1], a_part(q_y, x), a_part(q_y, x), sib)
+    for c in range(2):
+        send(ezy[c], a_part(q_y, c), e_part(q_y, c), mid_dev, ends, mids)
     recv(afwd[1], a_part(q_d, x))
     for o in range(3):
         aggregate(o, 1, 0)
@@ -410,11 +423,15 @@
         for s in range(4):
             dwf[s, rows, :] = acc[:, s * 128:(s + 1) * 128]
             dwp[s, rows, :] = acc[:, s * 128:(s + 1) * 128].astype(BF16)
+
+    def weight_send(h):
+        rows = pl.ds(h * 512, 512)
         for d in (2, 1, 3):
             to = (z + d) % 4
             send(dw_ids[h][d - 1], dwp.at[to, rows], dwr.at[z, rows], at(x, y, to, k))
 
     weight_grad(0)
+    weight_send(0)
     p_relay_y(1)
     send_layer_grad((3, 4, 5, 6))
     recv(b_ids[1], bsum.at[3])
@@ -422,10 +439,7 @@
     send(b_ids[2], bsum.at[4], bsum.at[5], sib)
     p_last(1)
     weight_grad(1)
-    for c in range(2):
-        recv(ez[c], e_part(q, c), mids)
-        send(ey[c], e_part(q, c), e_part(q, c), yn, mids, mids)
-        send(esib[c], e_part(q, c), e_part(q, c), sib, mids, mids)
+    weight_send(1)
     recv(b_ids[2], bsum.at[5])
     bsum[6] = bsum[4] + bsum[5]
     for d in (1, 2, 3):
@@ -436,8 +450,9 @@
             recv(i, dlq.at[xx * 4 + 2 * yy + kk], cond)
 
     f_in = [new() for _ in range(3)]
-    f_out = [new() for _ in range(2)]
-    f_fin = new()
+    f_out = [[new(), new()] for _ in range(2)]
+    f_fin = [new(), new()]
+    f_slices = (e2, m2, m)
     own_half = x == z // 2
 
     def grads(dl, a, scale, at_z, first, n, t, width):
@@ -465,53 +480,66 @@
             for i in range(n):
                 dff[first + i, :, cols] = acc[i * 128:(i + 1) * 128]
 
-    def grads_end(s):
-        @pl.loop(0, 4)
+    def grads_end(s, c):
+        @pl.loop(2 * c, 2 * c + 2)
         def _(t):
             acc, cols = grads(dle, adj_e, sbuf_e, e, s, 1, t, 512)
             tot = dff[s, :, cols] + acc
             dff[s, :, cols] = tot
             dfp[s, :, cols] = tot.astype(BF16)
 
-    layer_grads_here(mids)
-
-    @pl.when(mids)
-    def _():
-        grads_here(2 * pair, 2)
-        dfp[e] = dff[e].astype(BF16)
-    send(f_fin, dfp.at[e], fin.at[0], end_dev, mids, ends)
-
-    @pl.when(mids)
-    def _():
-        grads_here(2 * (1 - pair), 2)
-
-    def end_send():
-        layer_grads_here(ends)
-        for j, s in enumerate((m2, e2, m)):
-            send(f_in[j], dlq.at[:, s], dle.at[:, s], mid_dev, ends, mids)
+    def mid_pass():
+        recv(es, sbuf_e, mids)
+        for i, qq, on in ((ez, q, esib), (ezy, q_y, efwd)):
+            for c in range(2):
+                recv(i[c], e_part(qq, c), mids)
+                send(on[c], e_part(qq, c), e_part(qq, c), sib, mids, mids)
+
+    def end_send(j):
+        s = f_slices[j]
+        send(f_in[j], dlq.at[:, s], dle.at[:, s], mid_dev, ends, mids)
+
+    layer_grads_here(None)
+
+    def grads_own():
+        @pl.when(mids)
+        def _():
+            grads_here(2 * (1 - pair), 2)
+            grads_here(2 * pair, 2)
 
         @pl.when(ends)
         def _():
             grads_here(e, 1)
 
+
     def mid_ready():
-        recv(es, sbuf_e, mids)
-        for c in range(2):
-            recv(ey[c], e_part(q_y, c), mids)
-            send(efwd[c], e_part(q_y, c), e_part(q_y, c), sib, mids, mids)
         for c in range(2):
             recv(esib[c], e_part(q_s, c), mids)
             recv(efwd[c], e_part(q_d, c), mids)
 
+    def cut(c):
+        return pl.ds(c * 1024, 1024)
+
     def mid_send(j):
-        s_to = (m2, e2, m)[j]
+        s_to = f_slices[j]
         recv(f_in[j], dle.at[:, s_to], mids)
+        for c in range(2):
+            @pl.when(mids)
+            def _(c=c):
+                grads_end(s_to, c)
+            if j < 2:
+                send(f_out[j][c], dfp.at[s_to, :, cut(c)], fin.at[j, :, cut(c)],
+                     at(x, y, m2, k), mids, mids)
+
+    def mid_merge(c):
+        recv(f_out[0][c], fin.at[0, :, cut(c)], mids)
 
         @pl.when(mids)
         def _():
-            grads_end(s_to)
-        if j < 2:
-            send(f_out[j], dfp.at[s_to], fin.at[1], at(x, y, s_to, k), mids, (mids, ends)[j])
+            dfp[e, :, cut(c)] = (
+                dff[e, :, cut(c)] + fin[0, :, cut(c)].astype(F32)
+            ).astype(BF16)
+        send(f_fin[c], dfp.at[e, :, cut(c)], fin.at[1, :, cut(c)], end_dev, mids, ends)
 
     def piece(s, qq, c, h):
         return dw_ref.at[(s * 4 + qq) * 4 + c * 2 + h]
@@ -573,48 +601,24 @@
             line_send(gz, z_piece, d + 1, h)
         spread(h, d)
 
-    finish(0)
-    end_send()
-    mid_ready()
-    along(0, 1)
-    relay(0, 0)
-    finish(1)
-    along(0, 2)
-    relay(0, 1)
-    relay_diag(0, 0)
-    along(1, 1)
-    mid_send(0)
-    relay(1, 0)
-    relay_diag(0, 1)
-    along(0, 3)
-    mid_send(1)
-    relay(0, 2)
-    relay_diag(1, 0)
-    along(1, 2)
-    relay(1, 1)
-    relay_diag(0, 2)
-    along(1, 3)
-    mid_send(2)
-    relay(0, 3)
-    relay_diag(1, 1)
-    relay(1, 2)
-    relay_diag(0, 3)
-    relay(1, 3)
-    relay_diag(1, 2)
-    relay_diag(1, 3)
+    steps = {
+        "f": finish, "a": along, "r": relay, "d": relay_diag,
+        "E": end_send, "M": mid_send, "G": mid_merge, "R": mid_ready, "H": grads_own, "P": mid_pass,
+    }
+    for step in (t for group in ORDER for t in group.split()):
+        steps[step[0]](*(int(i) for i in step[1:]))
     for d in (1, 2, 3):
         recv(b_ids[2 + d], bsum.at[6 + d])
     db_ref[...] = bsum[6] + bsum[7] + bsum[8] + bsum[9]
 
-    recv(f_fin, fin.at[0], ends)
-    recv(f_out[0], fin.at[1], mids)
-    recv(f_out[1], fin.at[1], ends)
+    for c in range(2):
+        recv(f_out[1][c], fin.at[1, :, cut(c)], mids)
+        recv(f_fin[c], fin.at[1, :, cut(c)], ends)
 
     @pl.loop(0, 16)
     def _(t):
         cols = pl.ds(mult(t * 128, 128), 128)
-        first = jnp.where(ends, fin[0, :, cols].astype(F32), 0.0)
-        tot = dff[z, :, cols] + first + fin[1, :, cols].astype(F32)
+        tot = dff[z, :, cols] + fin[1, :, cols].astype(F32)
         dfeat_ref[pl.ds(mult(t * 128, 128), 128), :] = tot.T
 
     for o in range(4):
@@ -645,7 +649,7 @@
         c.wait()
 
 
-N_SEMS = 145
+N_SEMS = 148
 
 
 def per_device_fused(features, weight, bias, self_scale, adj_tiles, tile_ids, tile_counts, cotangent):

time: 146 us -> 136 us (0.932)
  the two profiles are of different devices: /device:TPU:0 before, /device:TPU:8 now
where the time goes in v5:
time: 136 us; the launch traced here: 134 us
  Pallas kernels  132 us (97%)
    pallas_call x1, Pallas kernels, per_device_fused(): pl.pallas_call(fused_kernel, out_shape=(pltpu.VMEM((128, 2048), F32), plt...  126 us
    pallas_call x1, Pallas kernels, per_device_fused(): pl.pallas_call(widen_kernel, out_shape=(jax.ShapeDtypeStruct((2048, 2048)...  6.62 us

profile of v5, /device:TPU:8, one launch (start us, length us, event | category | flops | bytes accessed | tf_op | source)
XLA Modules:
  0.0 133.7 jit_solution(15765755856586685294)
XLA Ops:
  1.3 125.7 %shard_map.111 = (f32[128,2048]{1,0:T(8,128)S(1)}, f32[2048,128]{1,0:T(8,128)S(1)}, bf16[64,128,512]{2,1,0:T(8,128)(2,1)S(1)}, f32[16,128]{1,0:T(8,128)S(1)}) custom-call(s32[32]{0:T(128)} %bitcast.11, s32[1]{0:T(128)} %bitcast.6.count_ref, bf16[32,128,128]{2,1,0:T(8,128)(2,1)} %bitcast.7, bf16[2048,128]{1,0:T(8,128)(2,1)} %feat_ref.1, ...), custom_call_target="tpu_custom_call" | custom-call | flops 7600000000 | bytes 25165824 | tf_op jit(solution)/shard_map/pallas_call | solution.py:659
  127.0 6.6 %shard_map.112 = (f32[2048,2048]{1,0:T(8,128)}, f32[128,2048]{1,0:T(8,128)}, f32[2048,128]{1,0:T(8,128)}, f32[16,128]{1,0:T(8,128)}) custom-call(bf16[64,128,512]{2,1,0:T(8,128)(2,1)S(1)} %get-tuple-element.12.dw_ref, f32[128,2048]{1,0:T(8,128)S(1)} %get-tuple-element.13.out_ref, f32[2048,128]{1,0:T(8,128)S(1)} %get-tuple-element.14.dfeat_ref, ...), custom_call_target="tpu_custom_call" | custom-call | tf_op jit(solution)/shard_map/pallas_call | solution.py:710

commit v6 on v5

--- a/solution.py
+++ b/solution.py
@@ -10,17 +10,19 @@
 BF16 = jnp.bfloat16
 MIB = 2**20
 ORDER = (
-    "H P f0 E0",
-    "a01 r00 R f1",
-    "E2 E1 a02 r01",
-    "d00 a11 M0 r10",
-    "d01 a03 M1 G0",
-    "r02 d10 a12 r03",
-    "r11 d02 a13 M2",
-    "d11 r12 d03 G1",
-    "r13 d12 d13",
+    "f0 W1 a01 r00",
+    "L H0 H1 f1",
+    "E0 a02 r01 P",
+    "R d00 a11 E1",
+    "r10 d01 M0 a03",
+    "E2 r02 d10 a12",
+    "G0 M1 r03 r11",
+    "d02 a13 G1 d11",
+    "r12 d03 M2 r13",
+    "d12 d13",
 )
 NC = 2
+PARTS = ((0, 512), (512, 512))
 
 
 def dense_block(tiles, ids, count, tile_rows, tile_cols):
@@ -69,9 +71,9 @@
 
 
 def fused_kernel(
-    ids_ref, count_ref, tiles_ref, feat_ref, w_ref, bias_ref, scale_ref, cot_ref,
+    ids_ref, count_ref, tiles_hbm, feat_ref, w_ref, bias_ref, scale_ref, cot_hbm,
     out_ref, dfeat_ref, dw_ref, db_ref,
-    adj, adj_e, hid, wv, sbuf, sbuf_e, scol, xs, xr, keep, lay, xrow, pre, pt, ptg, dls, dlq,
+    tiles_ref, cot_ref, adj, adj_e, hid, wv, sbuf, sbuf_e, scol, xs, xr, keep, lay, xrow, pre, pt, ptg, dls, dlq,
     dwf, dwp, dwr, dff, dfp, dle, fin, bsum, bias32, ssem, rsem, lsem,
 ):
     r = lax.axis_index("row")
@@ -142,7 +144,11 @@
 
     w_copy = pltpu.make_async_copy(w_ref, wv, lsem.at[0])
     h_copy = pltpu.make_async_copy(feat_ref, hid.at[z], lsem.at[1])
+    t_copy = pltpu.make_async_copy(tiles_hbm, tiles_ref, lsem.at[2])
+    c_copy = pltpu.make_async_copy(cot_hbm, cot_ref, lsem.at[3])
+    t_copy.start()
     h_copy.start()
+    t_copy.wait()
 
     for c in range(2):
         @pl.loop(0, 16)
@@ -160,6 +166,7 @@
     bias32[...] = bias_ref[...].astype(F32)
     h_copy.wait()
     w_copy.start()
+    c_copy.start()
     pl.semaphore_wait(barrier, jnp.where(ends, 4, 5))
 
     def h_part(s, c):
@@ -274,6 +281,7 @@
             recv(i, xrow.at[s * 4 + qq])
         if not w_waited:
             w_copy.wait()
+            c_copy.wait()
             w_waited.append(True)
         block = jnp.concatenate([xrow[s * 4 + i] for i in range(4)], axis=1)
 
@@ -327,12 +335,12 @@
     linear(3)
 
     def p_part(c, h):
-        return pt.at[pl.ds(mult(c * 1024 + h * 512, 512), 512)]
+        return pt.at[pl.ds(mult(c * 1024 + PARTS[h][0], 256), PARTS[h][1])]
 
     def activate(c, h):
-        @pl.loop(0, 4)
+        @pl.loop(PARTS[h][0] // 128, sum(PARTS[h]) // 128)
         def _(i):
-            t = c * 8 + h * 4 + i
+            t = c * 8 + i
             cols = pl.ds(mult(t * 128, 128), 128)
             v = pre[:, cols] + bias32[pl.ds(t, 1), :]
             sig = jax.nn.sigmoid(v)
@@ -343,17 +351,18 @@
             bsum[0, pl.ds(t, 1), :] = jnp.sum(d32, axis=0, keepdims=True)
 
     b_own, b_x = x * 4 + q, (1 - x) * 4 + q
-    px, py, pyf, ps, psf, pd, pdf = ([new(), new()] for _ in range(7))
+    px, py, pyf, ps, psf, pd, pdf = ([new() for _ in PARTS] for _ in range(7))
     b_ids = [new() for _ in range(6)]
 
     def p_at(b, h):
-        return ptg.at[b, pl.ds(h * 512, 512)]
+        return ptg.at[b, pl.ds(*PARTS[h])]
 
     def p_send(h):
         send(px[h], p_part(1 - x, h), p_at(b_own, h), xn)
         send(py[h], p_part(x, h), p_at(b_own, h), yn)
         send(ps[h], p_part(x, h), p_at(b_own, h), sib)
-        ptg[b_own, h * 512:(h + 1) * 512] = pt[pl.ds(mult(x * 1024 + h * 512, 512), 512), :]
+        first, n = PARTS[h]
+        ptg[b_own, first:first + n] = pt[pl.ds(mult(x * 1024 + first, 256), n), :]
 
     def p_relay_x(h):
         recv(px[h], p_at(b_x, h))
@@ -377,6 +386,10 @@
     p_send(0)
     activate(1 - x, 1)
     activate(x, 1)
+    if len(PARTS) > 2:
+        p_send(1)
+        activate(1 - x, 2)
+        activate(x, 2)
 
     @pl.loop(0, 2)
     def _(i):
@@ -399,7 +412,7 @@
             xx, yy, kk = dl_to[i]
             send(dl_ids[i], dls.at[2 * yy + kk], dlq.at[b_own], at(xx, yy, z, kk))
 
-    p_send(1)
+    p_send(len(PARTS) - 1)
     send(b_ids[0], bsum.at[0], bsum.at[1], xn)
     dlq[b_own] = dls[q]
     p_relay_x(0)
@@ -413,10 +426,10 @@
         recv(l_id[o], lay.at[slice_at(o), pl.ds(mult((1 - x) * 512, 512), 512)])
     p_last(0)
 
-    dw_ids = [[new() for _ in range(3)] for _ in range(2)]
+    dw_ids = [[new() for _ in range(5)] for _ in PARTS]
 
     def weight_grad(h):
-        rows = pl.ds(h * 512, 512)
+        rows = pl.ds(*PARTS[h])
         lhs = jnp.concatenate([ptg[b, rows, :] for b in range(8)], axis=1)
         rhs = jnp.concatenate([lay[s] for s in range(4)], axis=1)
         acc = jnp.dot(lhs, rhs, preferred_element_type=F32)
@@ -425,13 +438,29 @@
             dwp[s, rows, :] = acc[:, s * 128:(s + 1) * 128].astype(BF16)
 
     def weight_send(h):
-        rows = pl.ds(h * 512, 512)
-        for d in (2, 1, 3):
-            to = (z + d) % 4
-            send(dw_ids[h][d - 1], dwp.at[to, rows], dwr.at[z, rows], at(x, y, to, k))
+        rows = pl.ds(*PARTS[h])
+        for i, s_to in enumerate((m2, e2)):
+            send(dw_ids[h][i], dwp.at[s_to, rows], dwr.at[i, rows], mid_dev, ends, mids)
+        beside = at(x, y, m + e - z, k)
+        send(dw_ids[h][2], dwp.at[m + e - z, rows], dwr.at[2, rows], beside)
+
+    def weight_pass(h):
+        rows = pl.ds(*PARTS[h])
+        for i, s_to in enumerate((m2, e2)):
+            recv(dw_ids[h][i], dwr.at[i, rows], mids)
+
+            @pl.when(mids)
+            def _(i=i, s_to=s_to):
+                dwp[s_to, rows, :] = (
+                    dwf[s_to, rows, :] + dwr[i, rows, :].astype(F32)
+                ).astype(BF16)
+            send(dw_ids[h][3 + i], dwp.at[s_to, rows], dwr.at[3, rows],
+                 at(x, y, s_to, k), mids, (mids, ends)[i])
 
     weight_grad(0)
     weight_send(0)
+    if len(PARTS) > 2:
+        p_relay_x(2)
     p_relay_y(1)
     send_layer_grad((3, 4, 5, 6))
     recv(b_ids[1], bsum.at[3])
@@ -440,14 +469,21 @@
     p_last(1)
     weight_grad(1)
     weight_send(1)
+    weight_pass(0)
+    if len(PARTS) > 2:
+        p_relay_y(2)
+        p_last(2)
+        weight_grad(2)
+        weight_send(2)
+        weight_pass(1)
     recv(b_ids[2], bsum.at[5])
     bsum[6] = bsum[4] + bsum[5]
     for d in (1, 2, 3):
         send(b_ids[2 + d], bsum.at[6], bsum.at[6 + d], at(x, y, (z + d) % 4, k))
 
-    def layer_grads_here(cond):
+    def layer_grads_here():
         for i, (xx, yy, kk) in zip(dl_ids, dl_to):
-            recv(i, dlq.at[xx * 4 + 2 * yy + kk], cond)
+            recv(i, dlq.at[xx * 4 + 2 * yy + kk])
 
     f_in = [new() for _ in range(3)]
     f_out = [[new(), new()] for _ in range(2)]
@@ -499,17 +535,14 @@
         s = f_slices[j]
         send(f_in[j], dlq.at[:, s], dle.at[:, s], mid_dev, ends, mids)
 
-    layer_grads_here(None)
-
-    def grads_own():
+    def grads_own(i):
         @pl.when(mids)
         def _():
-            grads_here(2 * (1 - pair), 2)
-            grads_here(2 * pair, 2)
-
-        @pl.when(ends)
-        def _():
-            grads_here(e, 1)
+            grads_here(2 * (pair if i else 1 - pair), 2)
+        if i == 0:
+            @pl.when(ends)
+            def _():
+                grads_here(e, 1)
 
 
     def mid_ready():
@@ -542,24 +575,28 @@
         send(f_fin[c], dfp.at[e, :, cut(c)], fin.at[1, :, cut(c)], end_dev, mids, ends)
 
     def piece(s, qq, c, h):
-        return dw_ref.at[(s * 4 + qq) * 4 + c * 2 + h]
-
-    gz = tuple({(d, h): new() for d in (1, 2, 3) for h in (0, 1)} for _ in range(2))
-    gx, gy, gxy, gyx = ({(h, o): new() for h in (0, 1) for o in range(4)} for _ in range(4))
+        first, n = PARTS[h]
+        return dw_ref.at[pl.ds((s * 4 + qq) * 8 + c * 4 + first // 256, n // 256)]
+
+    gz = tuple({(d, h): new() for d in (1, 2, 3) for h in range(len(PARTS))} for _ in range(2))
+    gx, gy, gxy, gyx = (
+        {(h, o): new() for h in range(len(PARTS)) for o in range(4)} for _ in range(4)
+    )
     gs, gsd = ([new() for _ in range(4)] for _ in range(2))
 
     def z_piece(s, h):
         return piece(s, q, x, h)
 
     def finish(h):
-        for d in (1, 2, 3):
-            recv(dw_ids[h][d - 1], dwr.at[(z - d) % 4, pl.ds(h * 512, 512)])
-        for t in range(4):
-            rr = pl.ds(h * 512 + t * 128, 128)
-            tot = dwf[z, rr, :]
-            for d in (1, 2, 3):
-                tot = tot + dwr[(z + d) % 4, rr, :].astype(F32)
-            dw_ref[(z * 4 + q) * 4 + x * 2 + h, :, t * 128:(t + 1) * 128] = tot.T.astype(BF16)
+        rows = pl.ds(*PARTS[h])
+        recv(dw_ids[h][2], dwr.at[2, rows])
+        recv(dw_ids[h][3], dwr.at[3, rows], mids)
+        recv(dw_ids[h][4], dwr.at[3, rows], ends)
+        for t in range(PARTS[h][0] // 128, sum(PARTS[h]) // 128):
+            rr = pl.ds(t * 128, 128)
+            tot = dwf[z, rr, :] + dwr[2, rr, :].astype(F32) + dwr[3, rr, :].astype(F32)
+            half = t % 2 * 128
+            dw_ref[(z * 4 + q) * 8 + x * 4 + t // 2, :, half:half + 128] = tot.T.astype(BF16)
         line_send(gz, z_piece, 1, h)
         spread(h, 0)
 
@@ -569,17 +606,17 @@
         send(gy[h, o], src, src, yn)
 
     def whole(s, qq):
-        return dw_ref.at[pl.ds((s * 4 + qq) * 4, 4)]
+        return dw_ref.at[pl.ds((s * 4 + qq) * 8, 8)]
 
     def part(ref, i):
-        return ref.at[pl.ds(i * 64, 64)]
+        return ref.at[:, pl.ds(i * 64, 64)]
 
     def relay(h, o):
         s = slice_at(o)
         from_x, from_y = piece(s, q, 1 - x, h), piece(s, q_y, x, h)
         recv(gx[h, o], from_x)
         send(gxy[h, o], part(from_x, 0), part(from_x, 0), yn)
-        if h == 1:
+        if h == len(PARTS) - 1:
             send(gs[o], whole(s, q), whole(s, q), sib)
         recv(gy[h, o], from_y)
         send(gyx[h, o], part(from_y, 1), part(from_y, 1), xn)
@@ -588,7 +625,7 @@
         block = piece(slice_at(o), q_y, 1 - x, h)
         recv(gxy[h, o], part(block, 0))
         recv(gyx[h, o], part(block, 1))
-        if h == 1:
+        if h == len(PARTS) - 1:
             send(gsd[o], whole(slice_at(o), q_y), whole(slice_at(o), q_y), sib)
 
     def last(o):
@@ -604,6 +641,7 @@
     steps = {
         "f": finish, "a": along, "r": relay, "d": relay_diag,
         "E": end_send, "M": mid_send, "G": mid_merge, "R": mid_ready, "H": grads_own, "P": mid_pass,
+        "L": layer_grads_here, "W": weight_pass,
     }
     for step in (t for group in ORDER for t in group.split()):
         steps[step[0]](*(int(i) for i in step[1:]))
@@ -642,14 +680,14 @@
         for i in range(16)
     ]
     for i in range(16):
-        for j in range(4):
-            wide[i, :, j * 512:(j + 1) * 512] = dw_ref[4 * i + j].astype(F32)
+        for j in range(8):
+            wide[i, :, j * 256:(j + 1) * 256] = dw_ref[8 * i + j].astype(F32)
         rows[i].start()
     for c in copies + rows:
         c.wait()
 
 
-N_SEMS = 148
+N_SEMS = 152
 
 
 def per_device_fused(features, weight, bias, self_scale, adj_tiles, tile_ids, tile_counts, cotangent):
@@ -661,12 +699,14 @@
         out_shape=(
             pltpu.VMEM((128, 2048), F32),
             pltpu.VMEM((2048, 128), F32),
-            pltpu.VMEM((64, 128, 512), BF16),
+            pltpu.VMEM((128, 128, 256), BF16),
             pltpu.VMEM((16, 128), F32),
         ),
-        in_specs=[smem, smem, vmem, hbm, hbm, vmem, vmem, vmem],
+        in_specs=[smem, smem, hbm, hbm, hbm, vmem, vmem, hbm],
         out_specs=(vmem, vmem, vmem, vmem),
         scratch_shapes=[
+            pltpu.VMEM((32, 128, 128), BF16),
+            pltpu.VMEM((128, 2048), BF16),
             pltpu.VMEM((1024, 2048), BF16),
             pltpu.VMEM((1024, 2048), BF16),
             pltpu.VMEM((4, 2048, 128), BF16),
@@ -695,7 +735,7 @@
             pltpu.VMEM((16, 128), F32),
             pltpu.SemaphoreType.DMA((N_SEMS,)),
             pltpu.SemaphoreType.DMA((N_SEMS,)),
-            pltpu.SemaphoreType.DMA((3,)),
+            pltpu.SemaphoreType.DMA((4,)),
         ],
         compiler_params=pltpu.CompilerParams(
             collective_id=0, has_side_effects=True, vmem_limit_bytes=53 * MIB

time: 136 us -> 134 us (0.985); the launches traced: 134 us -> 134 us
  no operation moved by 1% of the time
where the time goes in v6:
time: 134 us
  Pallas kernels  133 us (99%)
  between operations  1.45 us (1%)
    pallas_call x1, Pallas kernels, per_device_fused(): pl.pallas_call(fused_kernel, out_shape=(pltpu.VMEM((128, 2048), F32), plt...  126 us
    pallas_call x1, Pallas kernels, per_device_fused(): pl.pallas_call(widen_kernel, out_shape=(jax.ShapeDtypeStruct((2048, 2048)...  6.62 us

profile of v6, /device:TPU:8, one launch (start us, length us, event | category | flops | bytes accessed | tf_op | source)
XLA Modules:
  0.0 134.3 jit_solution(10122845065873589493)
XLA Ops:
  1.3 126.2 %shard_map.111 = (f32[128,2048]{1,0:T(8,128)S(1)}, f32[2048,128]{1,0:T(8,128)S(1)}, bf16[128,128,256]{2,1,0:T(8,128)(2,1)S(1)}, f32[16,128]{1,0:T(8,128)S(1)}) custom-call(s32[32]{0:T(128)} %bitcast.11, s32[1]{0:T(128)} %bitcast.6.count_ref, bf16[32,128,128]{2,1,0:T(8,128)(2,1)} %bitcast.7, bf16[2048,128]{1,0:T(8,128)(2,1)} %feat_ref.1, ...), custom_call_target="tpu_custom_call" | custom-call | flops 7600000000 | bytes 25165824 | tf_op jit(solution)/shard_map/pallas_call | solution.py:697
  127.5 6.6 %shard_map.112 = (f32[2048,2048]{1,0:T(8,128)}, f32[128,2048]{1,0:T(8,128)}, f32[2048,128]{1,0:T(8,128)}, f32[16,128]{1,0:T(8,128)}) custom-call(bf16[128,128,256]{2,1,0:T(8,128)(2,1)S(1)} %get-tuple-element.12.dw_ref, f32[128,2048]{1,0:T(8,128)S(1)} %get-tuple-element.13.out_ref, f32[2048,128]{1,0:T(8,128)S(1)} %get-tuple-element.14.dfeat_ref, ...), custom_call_target="tpu_custom_call" | custom-call | tf_op jit(solution)/shard_map/pallas_call | solution.py:750

commit v7 on v6

--- a/solution.py
+++ b/solution.py
@@ -11,15 +11,15 @@
 MIB = 2**20
 ORDER = (
     "f0 W1 a01 r00",
-    "L H0 H1 f1",
-    "E0 a02 r01 P",
-    "R d00 a11 E1",
-    "r10 d01 M0 a03",
-    "E2 r02 d10 a12",
+    "L H0 r01 f1",
+    "a02 P H1 E0",
+    "R E1 d00 a11",
+    "r10 d01 M0 d10",
+    "a03 E2 r02 a12",
     "G0 M1 r03 r11",
-    "d02 a13 G1 d11",
-    "r12 d03 M2 r13",
-    "d12 d13",
+    "d02 a13 G1 d03",
+    "d11 r12 M2 r13",
+    "d13 d12",
 )
 NC = 2
 PARTS = ((0, 512), (512, 512))

time: 134 us -> 133 us (level)
  no operation moved by 1% of the time
where the time goes in v7:
time: 133 us
  Pallas kernels  132 us (99%)
  between operations  1.45 us (1%)
    pallas_call x1, Pallas kernels, per_device_fused(): pl.pallas_call(fused_kernel, out_shape=(pltpu.VMEM((128, 2048), F32), plt...  125 us
    pallas_call x1, Pallas kernels, per_device_fused(): pl.pallas_call(widen_kernel, out_shape=(jax.ShapeDtypeStruct((2048, 2048)...  6.62 us

profile of v7, /device:TPU:8, one launch (start us, length us, event | category | flops | bytes accessed | tf_op | source)
XLA Modules:
  0.0 133.2 jit_solution(7532198931581876518)
XLA Ops:
  1.3 125.1 %shard_map.111 = (f32[128,2048]{1,0:T(8,128)S(1)}, f32[2048,128]{1,0:T(8,128)S(1)}, bf16[128,128,256]{2,1,0:T(8,128)(2,1)S(1)}, f32[16,128]{1,0:T(8,128)S(1)}) custom-call(s32[32]{0:T(128)} %bitcast.11, s32[1]{0:T(128)} %bitcast.6.count_ref, bf16[32,128,128]{2,1,0:T(8,128)(2,1)} %bitcast.7, bf16[2048,128]{1,0:T(8,128)(2,1)} %feat_ref.1, ...), custom_call_target="tpu_custom_call" | custom-call | flops 7600000000 | bytes 25165824 | tf_op jit(solution)/shard_map/pallas_call | solution.py:697
  126.4 6.6 %shard_map.112 = (f32[2048,2048]{1,0:T(8,128)}, f32[128,2048]{1,0:T(8,128)}, f32[2048,128]{1,0:T(8,128)}, f32[16,128]{1,0:T(8,128)}) custom-call(bf16[128,128,256]{2,1,0:T(8,128)(2,1)S(1)} %get-tuple-element.12.dw_ref, f32[128,2048]{1,0:T(8,128)S(1)} %get-tuple-element.13.out_ref, f32[2048,128]{1,0:T(8,128)S(1)} %get-tuple-element.14.dfeat_ref, ...), custom_call_target="tpu_custom_call" | custom-call | tf_op jit(solution)/shard_map/pallas_call | solution.py:750

commit v8 on v7

--- a/solution.py
+++ b/solution.py
@@ -575,14 +575,12 @@
         send(f_fin[c], dfp.at[e, :, cut(c)], fin.at[1, :, cut(c)], end_dev, mids, ends)
 
     def piece(s, qq, c, h):
-        first, n = PARTS[h]
-        return dw_ref.at[pl.ds((s * 4 + qq) * 8 + c * 4 + first // 256, n // 256)]
+        return dw_ref.at[pl.ds((s * 4 + qq) * 8 + h * 4 + c * 2, 2)]
 
     gz = tuple({(d, h): new() for d in (1, 2, 3) for h in range(len(PARTS))} for _ in range(2))
-    gx, gy, gxy, gyx = (
-        {(h, o): new() for h in range(len(PARTS)) for o in range(4)} for _ in range(4)
+    gx, gy, gxy, gyx, gs, gsd = (
+        {(h, o): new() for h in range(len(PARTS)) for o in range(4)} for _ in range(6)
     )
-    gs, gsd = ([new() for _ in range(4)] for _ in range(2))
 
     def z_piece(s, h):
         return piece(s, q, x, h)
@@ -596,7 +594,8 @@
             rr = pl.ds(t * 128, 128)
             tot = dwf[z, rr, :] + dwr[2, rr, :].astype(F32) + dwr[3, rr, :].astype(F32)
             half = t % 2 * 128
-            dw_ref[(z * 4 + q) * 8 + x * 4 + t // 2, :, half:half + 128] = tot.T.astype(BF16)
+            at_block = (z * 4 + q) * 8 + h * 4 + x * 2 + t % 4 // 2
+            dw_ref[at_block, :, half:half + 128] = tot.T.astype(BF16)
         line_send(gz, z_piece, 1, h)
         spread(h, 0)
 
@@ -605,8 +604,8 @@
         send(gx[h, o], src, src, xn)
         send(gy[h, o], src, src, yn)
 
-    def whole(s, qq):
-        return dw_ref.at[pl.ds((s * 4 + qq) * 8, 8)]
+    def both(s, qq, h):
+        return dw_ref.at[pl.ds((s * 4 + qq) * 8 + h * 4, 4)]
 
     def part(ref, i):
         return ref.at[:, pl.ds(i * 64, 64)]
@@ -616,8 +615,7 @@
         from_x, from_y = piece(s, q, 1 - x, h), piece(s, q_y, x, h)
         recv(gx[h, o], from_x)
         send(gxy[h, o], part(from_x, 0), part(from_x, 0), yn)
-        if h == len(PARTS) - 1:
-            send(gs[o], whole(s, q), whole(s, q), sib)
+        send(gs[h, o], both(s, q, h), both(s, q, h), sib)
         recv(gy[h, o], from_y)
         send(gyx[h, o], part(from_y, 1), part(from_y, 1), xn)
 
@@ -625,12 +623,11 @@
         block = piece(slice_at(o), q_y, 1 - x, h)
         recv(gxy[h, o], part(block, 0))
         recv(gyx[h, o], part(block, 1))
-        if h == len(PARTS) - 1:
-            send(gsd[o], whole(slice_at(o), q_y), whole(slice_at(o), q_y), sib)
-
-    def last(o):
-        recv(gs[o], whole(slice_at(o), q_s))
-        recv(gsd[o], whole(slice_at(o), q_d))
+        send(gsd[h, o], both(slice_at(o), q_y, h), both(slice_at(o), q_y, h), sib)
+
+    def last(h, o):
+        recv(gs[h, o], both(slice_at(o), q_s, h))
+        recv(gsd[h, o], both(slice_at(o), q_d, h))
 
     def along(h, d):
         line_recv(gz, z_piece, d, h)
@@ -659,8 +656,9 @@
         tot = dff[z, :, cols] + fin[1, :, cols].astype(F32)
         dfeat_ref[pl.ds(mult(t * 128, 128), 128), :] = tot.T
 
-    for o in range(4):
-        last(o)
+    for h in range(len(PARTS)):
+        for o in range(4):
+            last(h, o)
     assert not pending and count[0] <= N_SEMS, count
     for i, (c, cond) in sent_by.items():
         when(cond, c.wait_send)
@@ -681,13 +679,14 @@
     ]
     for i in range(16):
         for j in range(8):
-            wide[i, :, j * 256:(j + 1) * 256] = dw_ref[8 * i + j].astype(F32)
+            block = 8 * i + j % 4 // 2 * 4 + j // 4 * 2 + j % 2
+            wide[i, :, j * 256:(j + 1) * 256] = dw_ref[block].astype(F32)
         rows[i].start()
     for c in copies + rows:
         c.wait()
 
 
-N_SEMS = 152
+N_SEMS = 160
 
 
 def per_device_fused(features, weight, bias, self_scale, adj_tiles, tile_ids, tile_counts, cotangent):

time: 133 us -> 134 us (level)
  no operation moved by 1% of the time
where the time goes in v8:
time: 134 us; the launch traced here: 133 us
  Pallas kernels  132 us (99%)
  between operations  1.45 us (1%)
    pallas_call x1, Pallas kernels, per_device_fused(): pl.pallas_call(fused_kernel, out_shape=(pltpu.VMEM((128, 2048), F32), plt...  125 us
    pallas_call x1, Pallas kernels, per_device_fused(): pl.pallas_call(widen_kernel, out_shape=(jax.ShapeDtypeStruct((2048, 2048)...  6.62 us

profile of v8, /device:TPU:8, one launch (start us, length us, event | category | flops | bytes accessed | tf_op | source)
XLA Modules:
  0.0 133.3 jit_solution(12098546228160875634)
XLA Ops:
  1.3 125.3 %shard_map.111 = (f32[128,2048]{1,0:T(8,128)S(1)}, f32[2048,128]{1,0:T(8,128)S(1)}, bf16[128,128,256]{2,1,0:T(8,128)(2,1)S(1)}, f32[16,128]{1,0:T(8,128)S(1)}) custom-call(s32[32]{0:T(128)} %bitcast.11, s32[1]{0:T(128)} %bitcast.6.count_ref, bf16[32,128,128]{2,1,0:T(8,128)(2,1)} %bitcast.7, bf16[2048,128]{1,0:T(8,128)(2,1)} %feat_ref.1, ...), custom_call_target="tpu_custom_call" | custom-call | flops 7600000000 | bytes 25165824 | tf_op jit(solution)/shard_map/pallas_call | solution.py:696
  126.5 6.6 %shard_map.112 = (f32[2048,2048]{1,0:T(8,128)}, f32[128,2048]{1,0:T(8,128)}, f32[2048,128]{1,0:T(8,128)}, f32[16,128]{1,0:T(8,128)}) custom-call(bf16[128,128,256]{2,1,0:T(8,128)(2,1)S(1)} %get-tuple-element.12.dw_ref, f32[128,2048]{1,0:T(8,128)S(1)} %get-tuple-element.13.out_ref, f32[2048,128]{1,0:T(8,128)S(1)} %get-tuple-element.14.dfeat_ref, ...), custom_call_target="tpu_custom_call" | custom-call | tf_op jit(solution)/shard_map/pallas_call | solution.py:749

commit v9 on v8

--- a/solution.py
+++ b/solution.py
@@ -459,10 +459,10 @@
 
     weight_grad(0)
     weight_send(0)
+    send_layer_grad((3, 4, 5, 6))
     if len(PARTS) > 2:
         p_relay_x(2)
     p_relay_y(1)
-    send_layer_grad((3, 4, 5, 6))
     recv(b_ids[1], bsum.at[3])
     bsum[4] = bsum[2] + bsum[3]
     send(b_ids[2], bsum.at[4], bsum.at[5], sib)

time: 134 us -> 134 us (level)
  no operation moved by 1% of the time
where the time goes in v9:
time: 134 us; the launch traced here: 133 us
  Pallas kernels  132 us (99%)
  between operations  1.45 us (1%)
    pallas_call x1, Pallas kernels, per_device_fused(): pl.pallas_call(fused_kernel, out_shape=(pltpu.VMEM((128, 2048), F32), plt...  125 us
    pallas_call x1, Pallas kernels, per_device_fused(): pl.pallas_call(widen_kernel, out_shape=(jax.ShapeDtypeStruct((2048, 2048)...  6.62 us

profile of v9, /device:TPU:8, one launch (start us, length us, event | category | flops | bytes accessed | tf_op | source)
XLA Modules:
  0.0 133.3 jit_solution(6321076559809090315)
XLA Ops:
  1.3 125.3 %shard_map.111 = (f32[128,2048]{1,0:T(8,128)S(1)}, f32[2048,128]{1,0:T(8,128)S(1)}, bf16[128,128,256]{2,1,0:T(8,128)(2,1)S(1)}, f32[16,128]{1,0:T(8,128)S(1)}) custom-call(s32[32]{0:T(128)} %bitcast.11, s32[1]{0:T(128)} %bitcast.6.count_ref, bf16[32,128,128]{2,1,0:T(8,128)(2,1)} %bitcast.7, bf16[2048,128]{1,0:T(8,128)(2,1)} %feat_ref.1, ...), custom_call_target="tpu_custom_call" | custom-call | flops 7600000000 | bytes 25165824 | tf_op jit(solution)/shard_map/pallas_call | solution.py:696
  126.5 6.6 %shard_map.112 = (f32[2048,2048]{1,0:T(8,128)}, f32[128,2048]{1,0:T(8,128)}, f32[2048,128]{1,0:T(8,128)}, f32[16,128]{1,0:T(8,128)}) custom-call(bf16[128,128,256]{2,1,0:T(8,128)(2,1)S(1)} %get-tuple-element.12.dw_ref, f32[128,2048]{1,0:T(8,128)S(1)} %get-tuple-element.13.out_ref, f32[2048,128]{1,0:T(8,128)S(1)} %get-tuple-element.14.dfeat_ref, ...), custom_call_target="tpu_custom_call" | custom-call | tf_op jit(solution)/shard_map/pallas_call | solution.py:749
